TPU v7x, 32 devices: a whole 2x2x4 slice. The times are simulated.
32 devices in a mesh: section: 2 (over core), dp: 4 (over z), tensor: 4 (over y, x).
Axes of the slice: x: 2, y: 2, z: 4, core: 2. Of those that a mesh axis runs over, the one named last changes fastest.
Arguments:
- tokens: bfloat16 [8, 1024, 1024], P('dp', 'tensor'), may hold values from -6 to 6
- cotangent: bfloat16 [8, 1024, 1024], P('dp', 'tensor'), may hold values from -6 to 6
- buckets: int32 [8], P('dp'), may hold values from 0 to 3, as said below
- lengths: int32 [8, 8], P('dp'), may hold values from 0 to 1024, as said below
- norm_gain_pairs: bfloat16 [2, 2, 1024], P('section'), may hold values from 0.25 to 1.75
- norm_bias_pairs: bfloat16 [2, 2, 1024], P('section'), may hold values from -1.796875 to 1.796875
- query_key_value_weight: bfloat16 [2, 1024, 3, 1024], P('section', None, None, 'tensor'), may hold values from -0.1875 to 0.1875
- query_value_bias: bfloat16 [2, 2, 1024], P('section', None, 'tensor'), may hold values from -1.796875 to 1.796875
- output_weight: bfloat16 [2, 1024, 1024], P('section', 'tensor'), may hold values from -0.75 to 0.75
- upward_weight: bfloat16 [2, 1024, 4096], P('section', None, 'tensor'), may hold values from -0.1875 to 0.1875
- upward_bias: bfloat16 [2, 4096], P('section', 'tensor'), may hold values from -1.796875 to 1.796875
- down_weight: bfloat16 [2, 4096, 1024], P('section', 'tensor'), may hold values from -0.09375 to 0.09375
- output_bias: bfloat16 [2, 2, 1024], P('section'), may hold values from -1.796875 to 1.796875
- adapter_down: bfloat16 [2, 2, 4, 1024], P('section'), may hold values from -0.1875 to 0.1875
- adapter_upper: bfloat16 [2, 2, 4, 1024], P('section', None, None, 'tensor'), may hold values from -0.23925781 to 0.23925781
Outputs:
- activations: bfloat16 [2, 8, 1024, 1024], P('section', 'dp', 'tensor')
- input_grad: bfloat16 [2, 8, 1024, 1024], P('section', 'dp', 'tensor')
- grad_lora_a: float32 [2, 2, 4, 1024], P('section')
- grad_lora_b: float32 [2, 2, 4, 1024], P('section', None, None, 'tensor')
Inputs may be any that keep to these rules, and one draw needn't show every extreme that they name: `buckets`: A micro-batch with bucket b holds items padded to 1024 / 2**(3 - b) rows; among the 2 micro-batches of each index of dp one at least has bucket 3. `lengths`: entry i of a micro-batch is item i's true length, more than half of its padded length and at most that; one item of each micro-batch fills its padded length; entries of items past the micro-batch's item count are 0.
All inputs are finite; a program needn't handle non-finite values.
Results may differ from a plain program's by a relative error of at most 0.028.
Values may be sent and summed in bfloat16 or wider, within the bound.
A program may use at most 128 MiB of HBM per device.

v0:
```python
from functools import partial

import jax
import jax.numpy as jnp
from jax import lax
from jax.sharding import PartitionSpec as P

HEAD_DIM = 64


adapter_scale = 8.0
norm_eps = 1e-05
masked_score = -1000000000.0
highest_precision = lax.Precision.HIGHEST


def from_behind(block, axis, distance):
    devices = range(lax.axis_size(axis))
    route = [(i - distance, i) for i in devices if i - distance in devices]
    return lax.ppermute(block, axis, route)


def layer_norm(values, gain_rows, shifts):
    center = jnp.mean(values, axis=-1, keepdims=True)
    centered = values - center
    spread = jnp.mean(centered * centered, axis=-1, keepdims=True)
    return centered * lax.rsqrt(spread + norm_eps) * gain_rows + shifts


def row_layout(bucket, lengths_row, row_count):
    item_span = jnp.right_shift(jnp.int32(row_count), 3 - bucket)
    positions = jnp.arange(row_count, dtype=jnp.int32)
    item_index = positions // item_span
    within = positions - item_index * item_span
    chosen = (
        item_index[:, None] == jnp.arange(lengths_row.shape[0], dtype=jnp.int32)[None, :]
    ).astype(jnp.int32)
    length = jnp.sum(chosen * lengths_row[None, :], axis=1)
    return (item_index, within < length)


def allowed_keys(item_index, is_valid):
    positions = jnp.arange(item_index.shape[0], dtype=jnp.int32)
    same_item = item_index[:, None] == item_index[None, :]
    causal = positions[None, :] <= positions[:, None]
    key_seen = is_valid[None, :] | (positions[None, :] == positions[:, None])
    return same_item & causal & key_seen


def take_slot(buffer, slot_index):
    return lax.dynamic_index_in_dim(buffer, slot_index, 0, keepdims=False)


def put_slot(buffer, slot_index, is_live, update):
    previous = take_slot(buffer, slot_index)
    return lax.dynamic_update_index_in_dim(
        buffer, jnp.where(is_live, update, previous), slot_index, 0
    )


def per_device(
    tokens,
    cotangent,
    buckets,
    lengths,
    norm_gain_pairs,
    norm_bias_pairs,
    query_key_value_weight,
    query_value_bias,
    output_weight,
    upward_weight,
    upward_bias,
    down_weight,
    output_bias,
    adapter_down,
    adapter_upper,
):
    section_index = lax.axis_index("section")
    tensor_count = lax.axis_size("tensor")
    micro_count, own_rows, model_width = tokens.shape
    row_count = own_rows * tensor_count
    own_start = lax.axis_index("tensor") * own_rows
    gain_sets = norm_gain_pairs[0].astype(jnp.float32)
    shift_sets = norm_bias_pairs[0].astype(jnp.float32)
    weight_qkv = query_key_value_weight[0]
    bias_query_value = query_value_bias[0].astype(jnp.float32)
    weight_out = output_weight[0]
    weight_up = upward_weight[0]
    bias_up = upward_bias[0].astype(jnp.float32)
    weight_down = down_weight[0]
    biases = output_bias[0].astype(jnp.float32)
    down_factor = adapter_down[0]
    upper_factor = adapter_upper[0]
    factor_wide = down_factor.astype(jnp.float32)
    local_width = weight_qkv.shape[2]
    local_heads = local_width // HEAD_DIM
    score_scale = HEAD_DIM ** (-0.5)

    def widen(values):
        return lax.all_gather(values, "tensor", axis=0, tiled=True)

    def widen_back(values):
        return lax.all_gather(values, "tensor", axis=0, tiled=True)

    def settle(source, weight):

        def row_term(first_row, row_span):
            return jnp.dot(source, weight, preferred_element_type=jnp.float32)

        return lax.psum_scatter(
            row_term(jnp.int32(0), lax.axis_size("tensor") * own_rows).astype(jnp.bfloat16),
            "tensor",
            scatter_dimension=0,
            tiled=True,
        ).astype(jnp.float32)

    def settle_back(row_term):
        return lax.psum_scatter(
            row_term(jnp.int32(0), lax.axis_size("tensor") * own_rows).astype(jnp.bfloat16),
            "tensor",
            scatter_dimension=0,
            tiled=True,
        ).astype(jnp.float32)

    def layout_of(slot_index):
        item_index, is_valid = row_layout(
            take_slot(buckets, slot_index), take_slot(lengths, slot_index), row_count
        )
        own_valid = lax.dynamic_slice_in_dim(is_valid, own_start, own_rows, 0)
        return (allowed_keys(item_index, is_valid), own_valid)

    def attend(normed, allowed):
        reduced_query = jnp.dot(
            normed, down_factor[0].T, preferred_element_type=jnp.float32
        ).astype(jnp.bfloat16)
        reduced_value = jnp.dot(
            normed, down_factor[1].T, preferred_element_type=jnp.float32
        ).astype(jnp.bfloat16)
        blended_rows = jnp.einsum(
            "rd,dcn->rcn", normed, weight_qkv, preferred_element_type=jnp.float32
        )
        query_matrix_rows = (
            blended_rows[:, 0]
            + bias_query_value[0]
            + adapter_scale
            * jnp.dot(reduced_query, upper_factor[0], preferred_element_type=jnp.float32)
        )
        value_matrix_rows = (
            blended_rows[:, 2]
            + bias_query_value[1]
            + adapter_scale
            * jnp.dot(reduced_value, upper_factor[1], preferred_element_type=jnp.float32)
        )
        packed = jnp.stack(
            [query_matrix_rows, blended_rows[:, 1], value_matrix_rows], axis=1
        ).astype(jnp.bfloat16)
        head_split = packed.reshape(row_count, 3, local_heads, HEAD_DIM)
        scores = (
            jnp.einsum(
                "qhe,khe->hqk",
                head_split[:, 0],
                head_split[:, 1],
                preferred_element_type=jnp.float32,
            )
            * score_scale
        )
        scores = jnp.where(allowed[None], scores, masked_score)
        top_score = jnp.max(scores, axis=-1, keepdims=True)
        exponent = jnp.exp(scores - top_score)
        attn_probs = exponent / jnp.sum(exponent, axis=-1, keepdims=True)
        return (reduced_query, reduced_value, head_split, attn_probs)

    def forward(hidden, allowed):
        normed = widen(layer_norm(hidden, gain_sets[0], shift_sets[0]).astype(jnp.bfloat16))
        reduced_query, reduced_value, head_split, attn_probs = attend(normed, allowed)
        probs_low = attn_probs.astype(jnp.bfloat16)
        mixed_heads = jnp.einsum(
            "hqk,khe->qhe", probs_low, head_split[:, 2], preferred_element_type=jnp.float32
        )
        attended = mixed_heads.reshape(row_count, local_width).astype(jnp.bfloat16)
        middle = hidden + (settle(attended, weight_out) + biases[0])
        normed_two = widen(layer_norm(middle, gain_sets[1], shift_sets[1]).astype(jnp.bfloat16))
        hidden_pre = jnp.dot(normed_two, weight_up, preferred_element_type=jnp.float32) + bias_up
        activated = jax.nn.gelu(hidden_pre, approximate=True).astype(jnp.bfloat16)
        output = middle + (settle(activated, weight_down) + biases[1])
        return (output, normed, middle, normed_two)

    def backward(hidden, grad_out, allowed, normed, middle, normed_two):
        reduced_query, reduced_value, head_split, attn_probs = attend(normed, allowed)
        probs_low = attn_probs.astype(jnp.bfloat16)
        hidden_pre = jnp.dot(normed_two, weight_up, preferred_element_type=jnp.float32) + bias_up
        grad_branch = widen_back(grad_out.astype(jnp.bfloat16))
        grad_act = jnp.einsum(
            "rd,fd->rf", grad_branch, weight_down, preferred_element_type=jnp.float32
        )
        gelu_pull = jax.vjp(partial(jax.nn.gelu, approximate=True), hidden_pre)[1]
        grad_pre = gelu_pull(grad_act)[0].astype(jnp.bfloat16)

        def mlp_term(first_row, row_span):
            return jnp.einsum("rf,df->rd", grad_pre, weight_up, preferred_element_type=jnp.float32)

        grad_norm_two = settle_back(mlp_term)
        second_pull = jax.vjp(
            partial(layer_norm, gain_rows=gain_sets[1], shifts=shift_sets[1]), middle
        )[1]
        grad_middle = grad_out + second_pull(grad_norm_two)[0]
        grad_attn = widen_back(grad_middle.astype(jnp.bfloat16))
        grad_heads = jnp.einsum(
            "rd,nd->rn", grad_attn, weight_out, preferred_element_type=jnp.float32
        )
        grad_heads = grad_heads.astype(jnp.bfloat16).reshape(row_count, local_heads, HEAD_DIM)
        grad_probs = jnp.einsum(
            "qhe,khe->hqk", grad_heads, head_split[:, 2], preferred_element_type=jnp.float32
        )
        grad_scores = attn_probs * (
            grad_probs - jnp.sum(attn_probs * grad_probs, axis=-1, keepdims=True)
        )
        grad_scores = grad_scores.astype(jnp.bfloat16)
        grad_query = (
            jnp.einsum(
                "hqk,khe->qhe", grad_scores, head_split[:, 1], preferred_element_type=jnp.float32
            )
            * score_scale
        )
        grad_key = (
            jnp.einsum(
                "hqk,qhe->khe", grad_scores, head_split[:, 0], preferred_element_type=jnp.float32
            )
            * score_scale
        )
        grad_value = jnp.einsum(
            "hqk,qhe->khe", probs_low, grad_heads, preferred_element_type=jnp.float32
        )
        grad_packed = (
            jnp.stack([grad_query, grad_key, grad_value], axis=1)
            .reshape(row_count, 3, local_width)
            .astype(jnp.bfloat16)
        )
        grad_pair = jnp.stack([grad_packed[:, 0], grad_packed[:, 2]])
        gradient_reduced = adapter_scale * jnp.einsum(
            "jrn,jkn->jrk", grad_pair, upper_factor, preferred_element_type=jnp.float32
        )

        def attn_term(first_row, row_span):
            dense_part = jnp.einsum(
                "rcn,dcn->rd", grad_packed, weight_qkv, preferred_element_type=jnp.float32
            )
            return dense_part + jnp.einsum(
                "jrk,jkd->rd", gradient_reduced, factor_wide, precision=highest_precision
            )

        grad_normed = settle_back(attn_term)
        first_pull = jax.vjp(
            partial(layer_norm, gain_rows=gain_sets[0], shifts=shift_sets[0]), hidden
        )[1]
        grad_hidden = grad_middle + first_pull(grad_normed)[0]
        grad_factor_a = jnp.einsum(
            "jrk,rd->jkd", gradient_reduced, normed.astype(jnp.float32), precision=highest_precision
        )
        gradient_upper_factor = adapter_scale * jnp.stack(
            [
                jnp.einsum(
                    "rk,rn->kn",
                    reduced_query,
                    grad_packed[:, 0],
                    preferred_element_type=jnp.float32,
                ),
                jnp.einsum(
                    "rk,rn->kn",
                    reduced_value,
                    grad_packed[:, 2],
                    preferred_element_type=jnp.float32,
                ),
            ]
        )
        return (grad_hidden, grad_factor_a, gradient_upper_factor)

    zero_rows = jnp.zeros((micro_count, own_rows, model_width), jnp.bfloat16)
    saved_start = ()

    def record(buffers, slot_index, is_live, layer_input, results):
        kept_in, outputs, saved = buffers
        output, normed, middle, normed_two = results
        low_output = output.astype(jnp.bfloat16)
        kept_in = put_slot(kept_in, slot_index, is_live, layer_input)
        outputs = put_slot(outputs, slot_index, is_live, low_output)
        return ((kept_in, outputs, saved), low_output)

    buffers = (zero_rows, zero_rows, saved_start)

    def run_phase(buffers, sources, phase_section):

        def phase_turn(slot_index, buffers):
            allowed, own_valid = layout_of(slot_index)
            layer_input = take_slot(sources, slot_index)
            results = forward(layer_input.astype(jnp.float32), allowed)
            return record(
                buffers, slot_index, section_index == phase_section, layer_input, results
            )[0]

        return lax.fori_loop(0, micro_count, phase_turn, buffers)

    buffers = run_phase(buffers, tokens, 0)
    received = from_behind(buffers[1], "section", 1)
    buffers = run_phase(buffers, received, 1)
    kept_in, outputs, saved = buffers

    def back_step(slot_index, grad_out, allowed):
        hidden = take_slot(kept_in, slot_index).astype(jnp.float32)
        output, normed, middle, normed_two = forward(hidden, allowed)
        return backward(hidden, grad_out, allowed, normed, middle, normed_two)

    def top_grad(slot_index, own_valid):
        return take_slot(cotangent, slot_index).astype(jnp.float32) * own_valid[:, None].astype(
            jnp.float32
        )

    zero_a = jnp.zeros(down_factor.shape, jnp.float32)
    zero_b = jnp.zeros(upper_factor.shape, jnp.float32)

    def run_back(loop_state, sources, phase_section):

        def phase_turn(slot_index, loop_state):
            grads_in, sum_a, sum_b = loop_state
            allowed, own_valid = layout_of(slot_index)
            if phase_section == 1:
                grad_out = top_grad(slot_index, own_valid)
            else:
                grad_out = take_slot(sources, slot_index).astype(jnp.float32)
            is_live = section_index == phase_section
            grad_hidden, grad_a, grad_b = back_step(slot_index, grad_out, allowed)
            grads_in = put_slot(grads_in, slot_index, is_live, grad_hidden.astype(jnp.bfloat16))
            sum_a = sum_a + jnp.where(is_live, grad_a, 0.0)
            sum_b = sum_b + jnp.where(is_live, grad_b, 0.0)
            return (grads_in, sum_a, sum_b)

        return lax.fori_loop(0, micro_count, phase_turn, loop_state)

    loop_state = run_back((zero_rows, zero_a, zero_b), zero_rows, 1)
    received_grads = from_behind(loop_state[0], "section", -1)
    grads_in, sum_a, sum_b = run_back(loop_state, received_grads, 0)
    total_a = lax.psum(sum_a, ("dp", "tensor"))
    total_b = lax.psum(sum_b, "dp")
    return (outputs[None], grads_in[None], total_a[None], total_b[None])


def solution(mesh):
    in_specs = (
        P("dp", "tensor", None),
        P("dp", "tensor", None),
        P("dp"),
        P("dp", None),
        P("section", None, None),
        P("section", None, None),
        P("section", None, None, "tensor"),
        P("section", None, "tensor"),
        P("section", "tensor", None),
        P("section", None, "tensor"),
        P("section", "tensor"),
        P("section", "tensor", None),
        P("section", None, None),
        P("section", None, None, None),
        P("section", None, None, "tensor"),
    )
    out_specs = (
        P("section", "dp", "tensor", None),
        P("section", "dp", "tensor", None),
        P("section", None, None, None),
        P("section", None, None, "tensor"),
    )
    return jax.shard_map(
        per_device, mesh=mesh, in_specs=in_specs, out_specs=out_specs, check_vma=False
    )
```

profile of v0, /device:TPU:0, one launch (start us, length us, event | category | flops | bytes accessed | tf_op | source)
XLA Modules:
  0.0 2414.9 jit_solution(14957275614924502017)
XLA Ops:
  14.0 393.4 %while.73 = (s32[]{:T(128)}, bf16[2,256,1024]{2,1,0:T(8,128)(2,1)S(1)}, bf16[2,256,1024]{2,1,0:T(8,128)(2,1)}, pred[]{:T(512)}, bf16[2,256,1024]{2,1,0:T(8,128)(...) while((s32[]{:T(128)}, ...), condition=%wide.region_10.11_spmd, body=%wide.region_0.10_spmd.sunk | while | flops 7594888704 | bytes 121302608 | solution.py:301
  19.1 36.1 %all-gather.16.cloned.1.call-done = bf16[1024,1024]{1,0:T(8,128)(2,1)} async-done(((bf16[256,1024]{1,0:T(8,128)(2,1)}), bf16[1024,1024]{1,0:T(8,128)(2,1)}) %all-gather.16.cloned.1.call-update) | async-done | bytes 2097168 | tf_op jit(solution)/shard_map/while/body/eval_jaxpr/all_gather | solution.py:100
  89.7 35.3 %reduce-scatter.11.cloned.1.call-done = bf16[256,1024]{1,0:T(8,128)(2,1)} async-done(((bf16[1024,1024]{1,0:T(8,128)(2,1)}), bf16[256,1024]{1,0:T(8,128)(2,1)}) %reduce-scatter.11.cloned.1.call-update) | async-done | bytes 524304 | tf_op jit(solution)/shard_map/while/body/eval_jaxpr/reduce_scatter | solution.py:110
  129.9 35.4 %all-gather.18.cloned.1.call-done = bf16[1024,1024]{1,0:T(8,128)(2,1)} async-done(((bf16[256,1024]{1,0:T(8,128)(2,1)}), bf16[1024,1024]{1,0:T(8,128)(2,1)}) %all-gather.18.cloned.1.call-update) | async-done | bytes 2097168 | tf_op jit(solution)/shard_map/while/body/eval_jaxpr/all_gather | solution.py:100
  284.9 35.3 %reduce-scatter.11.cloned.1.call-done = bf16[256,1024]{1,0:T(8,128)(2,1)} async-done(((bf16[1024,1024]{1,0:T(8,128)(2,1)}), bf16[256,1024]{1,0:T(8,128)(2,1)}) %reduce-scatter.11.cloned.1.call-update) | async-done | bytes 524304 | tf_op jit(solution)/shard_map/while/body/eval_jaxpr/reduce_scatter | solution.py:110
  325.0 35.4 %all-gather.18.cloned.1.call-done = bf16[1024,1024]{1,0:T(8,128)(2,1)} async-done(((bf16[256,1024]{1,0:T(8,128)(2,1)}), bf16[1024,1024]{1,0:T(8,128)(2,1)}) %all-gather.18.cloned.1.call-update) | async-done | bytes 2097168 | tf_op jit(solution)/shard_map/while/body/eval_jaxpr/all_gather | solution.py:100
  411.6 391.3 %while.74 = (s32[]{:T(128)}, bf16[2,256,1024]{2,1,0:T(8,128)(2,1)S(1)}, bf16[2,256,1024]{2,1,0:T(8,128)(2,1)}, pred[]{:T(512)}, bf16[2,256,1024]{2,1,0:T(8,128)(...) while((s32[]{:T(128)}, ...), condition=%wide.region_21.22_spmd, body=%wide.region_11.21_spmd.sunk | while | flops 7594888704 | bytes 121351824 | solution.py:301
  484.9 35.3 %reduce-scatter.15.cloned.1.call-done = bf16[256,1024]{1,0:T(8,128)(2,1)} async-done(((bf16[1024,1024]{1,0:T(8,128)(2,1)}), bf16[256,1024]{1,0:T(8,128)(2,1)}) %reduce-scatter.15.cloned.1.call-update) | async-done | bytes 524304 | tf_op jit(solution)/shard_map/while/body/eval_jaxpr/reduce_scatter | solution.py:110
  525.1 35.4 %all-gather.22.cloned.1.call-done = bf16[1024,1024]{1,0:T(8,128)(2,1)} async-done(((bf16[256,1024]{1,0:T(8,128)(2,1)}), bf16[1024,1024]{1,0:T(8,128)(2,1)}) %all-gather.22.cloned.1.call-update) | async-done | bytes 2097168 | tf_op jit(solution)/shard_map/while/body/eval_jaxpr/all_gather | solution.py:100
  680.4 35.3 %reduce-scatter.15.cloned.1.call-done = bf16[256,1024]{1,0:T(8,128)(2,1)} async-done(((bf16[1024,1024]{1,0:T(8,128)(2,1)}), bf16[256,1024]{1,0:T(8,128)(2,1)}) %reduce-scatter.15.cloned.1.call-update) | async-done | bytes 524304 | tf_op jit(solution)/shard_map/while/body/eval_jaxpr/reduce_scatter | solution.py:110
  720.6 35.4 %all-gather.22.cloned.1.call-done = bf16[1024,1024]{1,0:T(8,128)(2,1)} async-done(((bf16[256,1024]{1,0:T(8,128)(2,1)}), bf16[1024,1024]{1,0:T(8,128)(2,1)}) %all-gather.22.cloned.1.call-update) | async-done | bytes 2097168 | tf_op jit(solution)/shard_map/while/body/eval_jaxpr/all_gather | solution.py:100
  804.0 776.1 %while.76 = (s32[]{:T(128)}, bf16[2,256,1024]{2,1,0:T(8,128)(2,1)}, f32[2,4,1024]{2,1,0:T(4,128)S(1)}, f32[2,4,256]{2,1,0:T(4,128)S(1)}, pred[]{:T(512)}, /*inde...) while((s32[]{:T(128)}, bf16[2,256,1024]{2,1,0:T(8,128)(2,1)}, ...), condition=%wide.region_38.39_spmd.clone, body=%wide.region_22.38_spmd.clone.sunk | while | flops 14315255808 | bytes 378138560 | solution.py:337
  1015.4 35.3 %reduce-scatter.27.cloned.1.call-done = bf16[256,1024]{1,0:T(8,128)(2,1)} async-done(((bf16[1024,1024]{1,0:T(8,128)(2,1)}), bf16[256,1024]{1,0:T(8,128)(2,1)}) %reduce-scatter.27.cloned.1.call-update) | async-done | bytes 524304 | tf_op jit(solution)/shard_map/while/body/eval_jaxpr/reduce_scatter | solution.py:118
  1056.2 35.4 %all-gather.38.cloned.1.call-done = bf16[1024,1024]{1,0:T(8,128)(2,1)} async-done(((bf16[256,1024]{1,0:T(8,128)(2,1)}), bf16[1024,1024]{1,0:T(8,128)(2,1)}) %all-gather.38.cloned.1.call-update) | async-done | bytes 2097168 | tf_op jit(solution)/shard_map/while/body/eval_jaxpr/all_gather | solution.py:103
  1381.1 35.3 %reduce-scatter.27.cloned.1.call-done = bf16[256,1024]{1,0:T(8,128)(2,1)} async-done(((bf16[1024,1024]{1,0:T(8,128)(2,1)}), bf16[256,1024]{1,0:T(8,128)(2,1)}) %reduce-scatter.27.cloned.1.call-update) | async-done | bytes 524304 | tf_op jit(solution)/shard_map/while/body/eval_jaxpr/reduce_scatter | solution.py:118
  1421.9 35.4 %all-gather.38.cloned.1.call-done = bf16[1024,1024]{1,0:T(8,128)(2,1)} async-done(((bf16[256,1024]{1,0:T(8,128)(2,1)}), bf16[1024,1024]{1,0:T(8,128)(2,1)}) %all-gather.38.cloned.1.call-update) | async-done | bytes 2097168 | tf_op jit(solution)/shard_map/while/body/eval_jaxpr/all_gather | solution.py:103
  1585.9 736.6 %while.75 = (s32[]{:T(128)}, bf16[2,256,1024]{2,1,0:T(8,128)(2,1)}, f32[2,4,1024]{2,1,0:T(4,128)S(1)}, f32[2,4,256]{2,1,0:T(4,128)S(1)}, pred[]{:T(512)}, /*inde...) while((s32[]{:T(128)}, bf16[2,256,1024]{2,1,0:T(8,128)(2,1)}, ...), condition=%wide.region_55.56_spmd, body=%wide.region_39.55_spmd.sunk | while | flops 14313934848 | bytes 380231328 | solution.py:337
  1654.5 35.3 %reduce-scatter.19.cloned.1.call-done = bf16[256,1024]{1,0:T(8,128)(2,1)} async-done(((bf16[1024,1024]{1,0:T(8,128)(2,1)}), bf16[256,1024]{1,0:T(8,128)(2,1)}) %reduce-scatter.19.cloned.1.call-update) | async-done | bytes 524304 | tf_op jit(solution)/shard_map/while/body/eval_jaxpr/reduce_scatter | solution.py:110
  1777.5 35.3 %reduce-scatter.21.cloned.1.call-done = bf16[256,1024]{1,0:T(8,128)(2,1)} async-done(((bf16[1024,1024]{1,0:T(8,128)(2,1)}), bf16[256,1024]{1,0:T(8,128)(2,1)}) %reduce-scatter.21.cloned.1.call-update) | async-done | bytes 524304 | tf_op jit(solution)/shard_map/while/body/eval_jaxpr/reduce_scatter | solution.py:118
  1818.3 35.4 %all-gather.30.cloned.1.call-done = bf16[1024,1024]{1,0:T(8,128)(2,1)} async-done(((bf16[256,1024]{1,0:T(8,128)(2,1)}), bf16[1024,1024]{1,0:T(8,128)(2,1)}) %all-gather.30.cloned.1.call-update) | async-done | bytes 2097168 | tf_op jit(solution)/shard_map/while/body/eval_jaxpr/all_gather | solution.py:103
  2022.8 35.3 %reduce-scatter.19.cloned.1.call-done = bf16[256,1024]{1,0:T(8,128)(2,1)} async-done(((bf16[1024,1024]{1,0:T(8,128)(2,1)}), bf16[256,1024]{1,0:T(8,128)(2,1)}) %reduce-scatter.19.cloned.1.call-update) | async-done | bytes 524304 | tf_op jit(solution)/shard_map/while/body/eval_jaxpr/reduce_scatter | solution.py:110
  2145.8 35.3 %reduce-scatter.21.cloned.1.call-done = bf16[256,1024]{1,0:T(8,128)(2,1)} async-done(((bf16[1024,1024]{1,0:T(8,128)(2,1)}), bf16[256,1024]{1,0:T(8,128)(2,1)}) %reduce-scatter.21.cloned.1.call-update) | async-done | bytes 524304 | tf_op jit(solution)/shard_map/while/body/eval_jaxpr/reduce_scatter | solution.py:118
  2186.6 35.4 %all-gather.30.cloned.1.call-done = bf16[1024,1024]{1,0:T(8,128)(2,1)} async-done(((bf16[256,1024]{1,0:T(8,128)(2,1)}), bf16[1024,1024]{1,0:T(8,128)(2,1)}) %all-gather.30.cloned.1.call-update) | async-done | bytes 2097168 | tf_op jit(solution)/shard_map/while/body/eval_jaxpr/all_gather | solution.py:103
  2322.5 76.4 %psum.14 = f32[1,2,4,1024]{3,2,1,0:T(4,128)} all-reduce(f32[1,2,4,1024]{3,2,1,0:T(4,128)S(1)} %bitcast.1089), channel_id=1, replica_groups=mesh['section'=2,'dp'=4,'tensor'=4] {'dp','tensor'}, use_global_device_ids=true, to_apply=%region_56.57 | all-reduce | flops 8192 | bytes 65536 | tf_op jit(solution)/shard_map/psum | solution.py:342
  (673 shorter events, 1599.7 us)
Async XLA Ops:
  15.6 109.4 %reduce-scatter.11.cloned.1.call-start = ((), (), s32[]{:S(2)}) async-start(), calls=%async_computation.11 | async-start | bytes 2621440 | tf_op jit(solution)/shard_map/while/body/eval_jaxpr/reduce_scatter | solution.py:110
  129.8 79.8 %reduce-scatter.13.cloned.1.call-start = ((), (), s32[]{:S(2)}) async-start(), calls=%async_computation.13 | async-start | bytes 2621440 | tf_op jit(solution)/shard_map/while/body/eval_jaxpr/reduce_scatter | solution.py:110
  213.8 106.4 %reduce-scatter.11.cloned.1.call-start = ((), (), s32[]{:S(2)}) async-start(), calls=%async_computation.11 | async-start | bytes 2621440 | tf_op jit(solution)/shard_map/while/body/eval_jaxpr/reduce_scatter | solution.py:110
  325.0 79.9 %reduce-scatter.13.cloned.1.call-start = ((), (), s32[]{:S(2)}) async-start(), calls=%async_computation.13 | async-start | bytes 2621440 | tf_op jit(solution)/shard_map/while/body/eval_jaxpr/reduce_scatter | solution.py:110
  413.5 106.7 %reduce-scatter.15.cloned.1.call-start = ((), (), s32[]{:S(2)}) async-start(), calls=%async_computation.15 | async-start | bytes 2621440 | tf_op jit(solution)/shard_map/while/body/eval_jaxpr/reduce_scatter | solution.py:110
  525.1 79.9 %reduce-scatter.17.cloned.1.call-start = ((), (), s32[]{:S(2)}) async-start(), calls=%async_computation.17 | async-start | bytes 2621440 | tf_op jit(solution)/shard_map/while/body/eval_jaxpr/reduce_scatter | solution.py:110
  609.0 106.7 %reduce-scatter.15.cloned.1.call-start = ((), (), s32[]{:S(2)}) async-start(), calls=%async_computation.15 | async-start | bytes 2621440 | tf_op jit(solution)/shard_map/while/body/eval_jaxpr/reduce_scatter | solution.py:110
  720.6 79.9 %reduce-scatter.17.cloned.1.call-start = ((), (), s32[]{:S(2)}) async-start(), calls=%async_computation.17 | async-start | bytes 2621440 | tf_op jit(solution)/shard_map/while/body/eval_jaxpr/reduce_scatter | solution.py:110
  828.1 102.2 %reduce-scatter.25.cloned.1.call-start = ((), (), s32[]{:S(2)}) async-start(), calls=%async_computation.27 | async-start | bytes 2621440 | tf_op jit(solution)/shard_map/while/body/eval_jaxpr/reduce_scatter | solution.py:110
  897.0 107.6 %all-gather.36.cloned.1.call-start = ((), (), s32[]{:S(2)}) async-start(), calls=%async_computation.28 | async-start | bytes 2621440 | tf_op jit(solution)/shard_map/while/body/eval_jaxpr/all_gather | solution.py:100
  935.1 115.6 %reduce-scatter.27.cloned.1.call-start = ((), (), s32[]{:S(2)}) async-start(), calls=%async_computation.29 | async-start | bytes 2621440 | tf_op jit(solution)/shard_map/while/body/eval_jaxpr/reduce_scatter | solution.py:118
  1015.4 76.3 %all-gather.38.cloned.1.call-start = ((), (), s32[]{:S(2)}) async-start(), calls=%async_computation.30 | async-start | bytes 2621440 | tf_op jit(solution)/shard_map/while/body/eval_jaxpr/all_gather | solution.py:103
  1056.2 129.9 %reduce-scatter.29.cloned.1.call-start = ((), (), s32[]{:S(2)}) async-start(), calls=%async_computation.31 | async-start | bytes 2621440 | tf_op jit(solution)/shard_map/while/body/eval_jaxpr/reduce_scatter | solution.py:118
  1193.9 102.2 %reduce-scatter.25.cloned.1.call-start = ((), (), s32[]{:S(2)}) async-start(), calls=%async_computation.27 | async-start | bytes 2621440 | tf_op jit(solution)/shard_map/while/body/eval_jaxpr/reduce_scatter | solution.py:110
  1262.8 107.4 %all-gather.36.cloned.1.call-start = ((), (), s32[]{:S(2)}) async-start(), calls=%async_computation.28 | async-start | bytes 2621440 | tf_op jit(solution)/shard_map/while/body/eval_jaxpr/all_gather | solution.py:100
  1300.9 115.5 %reduce-scatter.27.cloned.1.call-start = ((), (), s32[]{:S(2)}) async-start(), calls=%async_computation.29 | async-start | bytes 2621440 | tf_op jit(solution)/shard_map/while/body/eval_jaxpr/reduce_scatter | solution.py:118
  1381.0 76.3 %all-gather.38.cloned.1.call-start = ((), (), s32[]{:S(2)}) async-start(), calls=%async_computation.30 | async-start | bytes 2621440 | tf_op jit(solution)/shard_map/while/body/eval_jaxpr/all_gather | solution.py:103
  1421.8 129.9 %reduce-scatter.29.cloned.1.call-start = ((), (), s32[]{:S(2)}) async-start(), calls=%async_computation.31 | async-start | bytes 2621440 | tf_op jit(solution)/shard_map/while/body/eval_jaxpr/reduce_scatter | solution.py:118
  1587.4 102.4 %reduce-scatter.19.cloned.1.call-start = ((), (), s32[]{:S(2)}) async-start(), calls=%async_computation.19 | async-start | bytes 2621440 | tf_op jit(solution)/shard_map/while/body/eval_jaxpr/reduce_scatter | solution.py:110
  1696.6 116.2 %reduce-scatter.21.cloned.1.call-start = ((), (), s32[]{:S(2)}) async-start(), calls=%async_computation.22 | async-start | bytes 2621440 | tf_op jit(solution)/shard_map/while/body/eval_jaxpr/reduce_scatter | solution.py:118
  1818.3 130.0 %reduce-scatter.23.cloned.1.call-start = ((), (), s32[]{:S(2)}) async-start(), calls=%async_computation.24 | async-start | bytes 2621440 | tf_op jit(solution)/shard_map/while/body/eval_jaxpr/reduce_scatter | solution.py:118
  1955.7 102.4 %reduce-scatter.19.cloned.1.call-start = ((), (), s32[]{:S(2)}) async-start(), calls=%async_computation.19 | async-start | bytes 2621440 | tf_op jit(solution)/shard_map/while/body/eval_jaxpr/reduce_scatter | solution.py:110
  2064.9 116.3 %reduce-scatter.21.cloned.1.call-start = ((), (), s32[]{:S(2)}) async-start(), calls=%async_computation.22 | async-start | bytes 2621440 | tf_op jit(solution)/shard_map/while/body/eval_jaxpr/reduce_scatter | solution.py:118
  2186.6 129.9 %reduce-scatter.23.cloned.1.call-start = ((), (), s32[]{:S(2)}) async-start(), calls=%async_computation.24 | async-start | bytes 2621440 | tf_op jit(solution)/shard_map/while/body/eval_jaxpr/reduce_scatter | solution.py:118
  (113 other events, 3454.4 us)
Sparse Core Ops, SparseCore 0:
  17.2 38.0 all-gather.15
  129.9 35.2 all-gather.17
  215.1 35.2 all-gather.15
  325.1 35.2 all-gather.17
  415.1 35.3 all-gather.19
  525.2 35.2 all-gather.21
  610.7 35.2 all-gather.19
  720.7 35.2 all-gather.21
  829.0 35.2 all-gather.33
  932.2 35.2 all-gather.31
  969.3 35.3 all-gather.35
  1056.3 35.3 all-gather.37
  1194.8 35.2 all-gather.33
  1297.9 35.2 all-gather.31
  1334.9 35.2 all-gather.35
  1422.0 35.3 all-gather.37
  1588.5 35.2 all-gather.23
  1694.8 35.2 all-gather.25
  1732.1 35.2 all-gather.27
  1818.4 35.2 all-gather.29
  1956.8 35.2 all-gather.23
  2063.1 35.3 all-gather.25
  2100.4 35.2 all-gather.27
  2186.7 35.2 all-gather.29
  (20 shorter events, 702.8 us)
where the time goes:
time: 2430 us; the launch traced here: 2410 us
  waiting for transfers between devices  1480 us (61%)
  matrix products  524 us (22%)
  other arithmetic  162 us (7%)
  local copies, waits for them, and re-layouts  88.5 us (4%)
  blocking collectives  85.5 us (4%)
  loops' own time  52.2 us (2%)
    all_gather x16, waiting for transfers between devices, widen(): return lax.all_gather(values, 'tensor', axis=0, tiled=True)  534 us
    reduce_scatter x12, waiting for transfers between devices, settle(): lax.psum_scatter(row_term(jnp.int32(0), lax.axis_size('tensor') * own_row...  415 us
    all_gather x8, waiting for transfers between devices, widen_back(): return lax.all_gather(values, 'tensor', axis=0, tiled=True)  268 us
    reduce_scatter x8, waiting for transfers between devices, settle_back(): lax.psum_scatter(row_term(jnp.int32(0), lax.axis_size('tensor') * own_row...  261 us
    sub x8, matrix products, attend(): exponent = jnp.exp(scores - top_score)  88.6 us
    psum x1, blocking collectives, per_device(): total_a = lax.psum(sum_a, ('dp', 'tensor'))  76.4 us
    dot_general x12, matrix products, row_term(): return jnp.dot(source, weight, preferred_element_type=jnp.float32)  61.3 us
    dot_general x8, matrix products, forward(): jnp.einsum('hqk,khe->qhe', probs_low, head_split[:, 2], preferred_element...  59.5 us
  transfers between devices with their start and end apart: 46, of which 46 were waited for; matrix products, arithmetic and copies ran while one was open for 4% of the time, Pallas kernels for 0%

commit v1 on v0

--- a/solution.py
+++ b/solution.py
@@ -3,6 +3,8 @@
 import jax
 import jax.numpy as jnp
 from jax import lax
+from jax.experimental import pallas as pl
+from jax.experimental.pallas import tpu as pltpu
 from jax.sharding import PartitionSpec as P
 
 HEAD_DIM = 64
@@ -344,6 +346,790 @@
     return (outputs[None], grads_in[None], total_a[None], total_b[None])
 
 
+R = 256
+D = 1024
+NEG = -1e30
+F32 = jnp.float32
+BF16 = jnp.bfloat16
+MESH = pl.DeviceIdType.MESH
+CHUNK = 32
+
+
+def nn(a, b):
+    return lax.dot_general(a, b, (((1,), (0,)), ((), ())), preferred_element_type=F32)
+
+
+def nt(a, b):
+    return lax.dot_general(a, b, (((1,), (1,)), ((), ())), preferred_element_type=F32)
+
+
+def tn(a, b):
+    return lax.dot_general(a, b, (((0,), (0,)), ((), ())), preferred_element_type=F32)
+
+
+def normalize(v):
+    centered = v - jnp.mean(v, axis=-1, keepdims=True)
+    rs = lax.rsqrt(jnp.mean(centered * centered, axis=-1, keepdims=True) + norm_eps)
+    return centered * rs, rs
+
+
+def norm_pull(v, g):
+    xhat, rs = normalize(v)
+    return rs * (
+        g
+        - jnp.mean(g, axis=-1, keepdims=True)
+        - xhat * jnp.mean(g * xhat, axis=-1, keepdims=True)
+    )
+
+
+def gelu_pair(z):
+    c = 0.7978845608028654
+    z2 = z * z
+    t = jnp.tanh(c * (z + 0.044715 * (z2 * z)))
+    half = 0.5 * (1.0 + t)
+    slope = half + (0.5 * c) * z * (1.0 - t * t) * (1.0 + (3.0 * 0.044715) * z2)
+    return z * half, slope
+
+
+def fused_kernel(
+    tok, cot, buckets, lengths, small_in, wq_in, wo_in, wu_in, wd_in,
+    act, ig, ga, gb,
+    SP, WQ, WO, WU, WD, H, DY, MID, GP, Q, KV, OT, LSE, SND, RCV, ACC, ST, MSK,
+    DKV, DR, DQ, DOT, DO, AB, U, OACC,
+    tok_sem, tok_snd, wsem, wloc, wsib, wy, wfwd, kv_rcv, kv_snd, x_rcv, x_snd,
+    dr_rcv, dr_snd, out_rcv, out_snd,
+):
+    s = lax.axis_index("section")
+    d = lax.axis_index("dp")
+    t = lax.axis_index("tensor")
+    x = lax.rem(t, 2)
+    y = lax.div(t, 2)
+    sib = (1 - s, d, t)
+    xp = (s, d, y * 2 + 1 - x)
+    yp = (s, d, (1 - y) * 2 + x)
+    flip = s + x - 2 * s * x
+    own_i = flip
+
+    def blk_of(i):
+        return 2 * i + (s + i - 2 * s * i)
+
+    bar = pltpu.get_barrier_semaphore()
+    for ds_ in range(2):
+        for dx in range(2):
+            for dy in range(2):
+                if ds_ or dx or dy:
+                    s2 = 1 - s if ds_ else s
+                    x2 = 1 - x if dx else x
+                    y2 = 1 - y if dy else y
+                    pl.semaphore_signal(bar, 1, device_id=(s2, d, y2 * 2 + x2), device_id_type=MESH)
+    pl.semaphore_wait(bar, 7)
+
+    my_core = x + y - 2 * x * y
+
+    def spread(src, dst, which):
+        @pl.when(s == my_core)
+        def _():
+            for k, (dx, dy) in enumerate(((1, 0), (0, 1), (1, 1))):
+                x2 = 1 - x if dx else x
+                y2 = 1 - y if dy else y
+                pltpu.make_async_remote_copy(
+                    src.at[y2], dst.at[y], tok_snd.at[which, k], tok_sem.at[which, y],
+                    device_id=(s, d, y2 * 2 + x2), device_id_type=MESH,
+                ).start()
+            pltpu.make_async_copy(src.at[y], dst.at[y], tok_sem.at[which, y]).start()
+
+    def spread_done(src, dst, which):
+        @pl.when(s == my_core)
+        def _():
+            for k, (dx, dy) in enumerate(((1, 0), (0, 1), (1, 1))):
+                x2 = 1 - x if dx else x
+                y2 = 1 - y if dy else y
+                pltpu.make_async_remote_copy(
+                    src.at[y2], dst.at[y], tok_snd.at[which, k], tok_sem.at[which, y],
+                    device_id=(s, d, y2 * 2 + x2), device_id_type=MESH,
+                ).wait_send()
+
+    pieces = ((small_in, SP), (wq_in, WQ), (wo_in, WO), (wu_in, WU), (wd_in, WD))
+
+    def w_local(p):
+        src, dst = pieces[p]
+        return pltpu.make_async_copy(src, dst.at[s, y], wsem.at[s, y, p])
+
+    def w_sib(p):
+        src, dst = pieces[p]
+        return pltpu.make_async_remote_copy(
+            src, dst.at[s, y], wsib.at[p], wsem.at[s, y, p], device_id=sib, device_id_type=MESH)
+
+    def w_y(p):
+        src, dst = pieces[p]
+        return pltpu.make_async_remote_copy(
+            src, dst.at[s, y], wy.at[p], wsem.at[s, y, p], device_id=yp, device_id_type=MESH)
+
+    def w_forward(p):
+        dst = pieces[p][1]
+        return pltpu.make_async_remote_copy(
+            dst.at[s, 1 - y], dst.at[s, 1 - y], wfwd.at[p], wsem.at[s, 1 - y, p],
+            device_id=sib, device_id_type=MESH)
+
+    def w_wait(l, j, p):
+        src, dst = pieces[p]
+        pltpu.make_async_copy(src, dst.at[l, j], wsem.at[l, j, p]).wait()
+
+    def w_ready(l, p):
+        w_wait(l, 0, p)
+        w_wait(l, 1, p)
+
+        @pl.when(l == s)
+        def _():
+            w_forward(p).start()
+
+    spread(tok, H.at[0], 0)
+    for p in range(2):
+        w_local(p).start()
+        w_sib(p).start()
+
+        @pl.when(s == 0)
+        def _():
+            w_y(p).start()
+    for p in range(2, 5):
+        w_local(p).start()
+        w_sib(p).start()
+
+        @pl.when(s == 0)
+        def _():
+            w_y(p).start()
+
+    shift = 7 + buckets[y]
+    span_mask = lax.shift_left(jnp.int32(1), shift) - 1
+
+    def length_of(pos):
+        item = lax.shift_right_logical(pos, jnp.broadcast_to(shift, pos.shape))
+        got = jnp.zeros(pos.shape, jnp.int32)
+        for k in range(lengths.shape[1]):
+            got = jnp.where(item == k, lengths[y, k], got)
+        return item, jnp.bitwise_and(pos, span_mask) < got
+
+    def build_mask(i):
+        b = blk_of(i)
+        q_row = b * R + lax.broadcasted_iota(jnp.int32, (1, R), 1)
+        q_item = lax.shift_right_logical(q_row, jnp.broadcast_to(shift, q_row.shape))
+
+        def rows(r, carry):
+            r0 = pl.multiple_of(r * CHUNK, CHUNK)
+            k_row = r0 + lax.broadcasted_iota(jnp.int32, (CHUNK, 1), 0)
+            k_item, k_ok = length_of(k_row)
+            k_tag = jnp.where(k_ok, k_item, -1)
+            same = (k_tag == q_item) & (k_row <= q_row)
+            allowed = same | (k_row == q_row)
+            MSK[i, pl.ds(r0, CHUNK), :] = jnp.where(allowed, 0.0, NEG).astype(BF16)
+            return carry
+
+        lax.fori_loop(0, (b + 1) * (R // CHUNK), rows, 0)
+
+    build_mask(0)
+    build_mask(1)
+    ga[...] = jnp.zeros(ga.shape, F32)
+    gb[...] = jnp.zeros(gb.shape, F32)
+
+    def x_copy(slot, i):
+        return pltpu.make_async_remote_copy(
+            SND.at[slot, i], RCV.at[slot, i], x_snd.at[slot, i], x_rcv.at[slot, i],
+            device_id=xp, device_id_type=MESH)
+
+    def by_rows(body, step=CHUNK):
+        def turn(r, carry):
+            body(pl.ds(pl.multiple_of(r * step, step), step))
+            return carry
+
+        lax.fori_loop(0, R // step, turn, 0)
+
+    def swapped(slot, i, rows):
+        return SND[slot, i, rows, :].astype(F32) + RCV[slot, i, rows, :].astype(F32)
+
+    def send_result(which, layer, src):
+        dst = act if which < 2 else ig
+        o = 0 if which < 2 else 1
+        here = (s == layer) & (y == own_i)
+
+        @pl.when(here)
+        def _():
+            pltpu.make_async_copy(src, dst.at[y], out_rcv.at[o, y]).start()
+
+        @pl.when(jnp.logical_not(here))
+        def _():
+            pltpu.make_async_remote_copy(
+                src, dst.at[y], out_snd.at[which], out_rcv.at[o, y],
+                device_id=(layer, d, own_i * 2 + x), device_id_type=MESH).start()
+
+    def send_result_done(which, layer, src):
+        dst = act if which < 2 else ig
+        o = 0 if which < 2 else 1
+        here = (s == layer) & (y == own_i)
+
+        @pl.when(jnp.logical_not(here))
+        def _():
+            pltpu.make_async_remote_copy(
+                src, dst.at[y], out_snd.at[which], out_rcv.at[o, y],
+                device_id=(layer, d, own_i * 2 + x), device_id_type=MESH).wait_send()
+
+    def vec(l, k):
+        return SP[l, 0, k : k + 1, :]
+
+    def head_lanes(pair):
+        return pl.ds(pl.multiple_of(pair * 128, 128), 128)
+
+    def split_pair(v, axis):
+        which = lax.broadcasted_iota(jnp.int32, v.shape, axis) < HEAD_DIM
+        zero = jnp.zeros_like(v)
+        return jnp.where(which, v, zero), jnp.where(which, zero, v)
+
+    def kv_copy(l, i):
+        rows = pl.ds(pl.multiple_of(blk_of(i) * R, R), R)
+        return pltpu.make_async_remote_copy(
+            KV.at[l, :, rows, :], KV.at[l, :, rows, :], kv_snd.at[l, i], kv_rcv.at[l, i],
+            device_id=sib, device_id_type=MESH)
+
+    def kv_wait(l, i):
+        b = 2 * i + (1 - s + i - 2 * (1 - s) * i)
+        rows = pl.ds(pl.multiple_of(b * R, R), R)
+        pltpu.make_async_remote_copy(
+            KV.at[l, :, rows, :], KV.at[l, :, rows, :], kv_snd.at[l, i], kv_rcv.at[l, i],
+            device_id=sib, device_id_type=MESH).wait_recv()
+
+    def attend(l, i):
+        b = blk_of(i)
+
+        def pair_turn(pair, carry):
+            lanes = head_lanes(pair)
+            qs = split_pair(Q[l, i, :, lanes], 1)
+
+            def first(j, tops):
+                rows = pl.ds(pl.multiple_of(j * R, R), R)
+                keys = KV[l, 0, rows, lanes]
+                mask = MSK[i, rows, :].astype(F32)
+                new = []
+                for e in range(2):
+                    st = nt(keys, qs[e]) + mask
+                    ST[e, rows, :] = st
+                    new.append(jnp.maximum(tops[e], jnp.max(st, axis=0, keepdims=True)))
+                return tuple(new)
+
+            tops = lax.fori_loop(0, b + 1, first, (jnp.full((1, R), NEG, F32),) * 2)
+            OACC[...] = jnp.zeros(OACC.shape, F32)
+
+            def second(j, sums):
+                rows = pl.ds(pl.multiple_of(j * R, R), R)
+                values = KV[l, 1, rows, lanes]
+                new = []
+                for e in range(2):
+                    p = jnp.exp(ST[e, rows, :] - tops[e])
+                    new.append(sums[e] + jnp.sum(p, axis=0, keepdims=True))
+                    OACC[e] += tn(values, p.astype(BF16))
+                return tuple(new)
+
+            sums = lax.fori_loop(0, b + 1, second, (jnp.zeros((1, R), F32),) * 2)
+            for e in range(2):
+                OT[l, i, pl.ds(pl.multiple_of(pair * 128 + e * 64, 64), 64), :] = (
+                    OACC[e, e * 64 : e * 64 + 64, :] * (1.0 / sums[e])
+                ).astype(BF16)
+                LSE[l, i, pair * 2 + e] = tops[e] + jnp.log(sums[e])
+            return carry
+
+        lax.fori_loop(0, Q.shape[3] // 128, pair_turn, 0)
+
+    def forward_attention(l, i):
+        b = blk_of(i)
+
+        @pl.when(i == 0)
+        def _():
+            w_ready(l, 0)
+            w_ready(l, 1)
+
+        @pl.when(l == 0)
+        def _():
+            pltpu.make_async_copy(tok.at[0], H.at[0, i], tok_sem.at[0, i]).wait()
+
+        @pl.when(l == 1)
+        def _():
+            x_copy(1, i).wait_recv()
+
+            def rows_in(rows):
+                h = MID[0, i, rows, :] + (swapped(1, i, rows) + vec(0, 5))
+                H[1, i, rows, :] = h.astype(BF16)
+
+            by_rows(rows_in)
+
+            @pl.when(i == own_i)
+            def _():
+                send_result(0, 0, H.at[1, i])
+
+        def rows_norm(rows):
+            xhat, _ = normalize(H[l, i, rows, :].astype(F32))
+            AB[rows, :] = (xhat * vec(l, 0) + vec(l, 1)).astype(BF16)
+
+        by_rows(rows_norm)
+        u = nt(AB[...], SP[l, 0, 8:16, :].astype(BF16)).astype(BF16)
+        U[l, i] = u
+        own_rows = pl.ds(pl.multiple_of(b * R, R), R)
+        for j in range(2):
+            up = SP[l, j, 24:32, 0:768].astype(BF16)
+            qkv = nn(AB[...], WQ[l, j]) + (adapter_scale * nn(u, up) + SP[l, j, 17:18, 0:768])
+            cols = slice(j * 256, j * 256 + 256)
+            Q[l, i, :, cols] = (qkv[:, 0:256] * HEAD_DIM ** -0.5).astype(BF16)
+            KV[l, 0, own_rows, cols] = qkv[:, 256:512].astype(BF16)
+            KV[l, 1, own_rows, cols] = qkv[:, 512:768].astype(BF16)
+
+        @pl.when(b != 3)
+        def _():
+            kv_copy(l, i).start()
+
+        @pl.when((s == 1) & (i == 0))
+        def _():
+            kv_wait(l, 0)
+
+        @pl.when((s == 0) & (i == 1))
+        def _():
+            kv_wait(l, 0)
+            kv_wait(l, 1)
+
+        attend(l, i)
+
+        @pl.when(i == 0)
+        def _():
+            w_ready(l, 2)
+
+        @pl.when(l == 1)
+        def _():
+            x_copy(0, i).wait_send()
+
+        SND[0, i] = (tn(OT[l, i, 0:256, :], WO[l, 0]) + tn(OT[l, i, 256:512, :], WO[l, 1])).astype(BF16)
+        x_copy(0, i).start()
+
+    def forward_ff(l, i):
+        @pl.when(i == 0)
+        def _():
+            @pl.when((s == 1) & (l == 0))
+            def _():
+                for p in range(5):
+                    w_y(p).start()
+
+            w_ready(l, 3)
+            w_ready(l, 4)
+
+        x_copy(0, i).wait_recv()
+
+        def rows_mid(rows):
+            mid = H[l, i, rows, :].astype(F32) + (swapped(0, i, rows) + vec(l, 4))
+            MID[l, i, rows, :] = mid
+            xhat, _ = normalize(mid)
+            AB[rows, :] = (xhat * vec(l, 2) + vec(l, 3)).astype(BF16)
+
+        by_rows(rows_mid)
+        for n in range(4):
+            j, half = n // 2, n % 2
+            cols = slice(half * 512, half * 512 + 512)
+            z = nn(AB[...], WU[l, j, :, cols]) + SP[l, j, 16:17, cols]
+            g, slope = gelu_pair(z)
+            GP[l, i, :, n * 512 : n * 512 + 512] = slope.astype(BF16)
+            term = nn(g.astype(BF16), WD[l, j, cols, :])
+            if n == 0:
+                ACC[...] = term
+            else:
+                ACC[...] += term
+        slot = 1 + l
+        SND[slot, i] = ACC[...].astype(BF16)
+
+        @pl.when(l == 0)
+        def _():
+            x_copy(1, i).start()
+
+        @pl.when((l == 1) & (i != own_i))
+        def _():
+            x_copy(2, i).start()
+
+    def fwd_layer(l, carry):
+        @pl.when(l == 1)
+        def _():
+            spread(cot, DY, 1)
+
+        def a_turn(i, c):
+            forward_attention(l, i)
+            return c
+
+        def f_turn(i, c):
+            forward_ff(l, i)
+            return c
+
+        lax.fori_loop(0, 2, a_turn, 0)
+        lax.fori_loop(0, 2, f_turn, 0)
+        return carry
+
+    lax.fori_loop(0, 2, fwd_layer, 0)
+
+    def finish_forward():
+        x_copy(2, own_i).wait_recv()
+
+        def rows_out(rows):
+            out = MID[1, own_i, rows, :] + (swapped(2, own_i, rows) + vec(1, 5))
+            SND[2, own_i, rows, :] = out.astype(BF16)
+
+        by_rows(rows_out)
+        send_result(1, 1, SND.at[2, own_i])
+
+    def backward_ff(l, i):
+        @pl.when(l == 1)
+        def _():
+            pltpu.make_async_copy(cot.at[0], DY.at[i], tok_sem.at[1, i]).wait()
+
+            def rows_valid(rows):
+                pos = blk_of(i) * R + rows.start + lax.broadcasted_iota(jnp.int32, (CHUNK, 1), 0)
+                _, ok = length_of(pos)
+                DY[i, rows, :] = (DY[i, rows, :].astype(F32) * jnp.where(ok, 1.0, 0.0)).astype(BF16)
+
+            by_rows(rows_valid)
+
+        @pl.when(l == 0)
+        def _():
+            x_copy(0, i).wait_recv()
+
+            def rows_in(rows):
+                g = swapped(0, i, rows) * vec(1, 0)
+                DY[i, rows, :] = (MID[1, i, rows, :] + norm_pull(H[1, i, rows, :].astype(F32), g)).astype(BF16)
+
+            by_rows(rows_in)
+
+            @pl.when(i == own_i)
+            def _():
+                send_result(2, 1, DY.at[i])
+
+        for n in range(4):
+            j, half = n // 2, n % 2
+            cols = slice(half * 512, half * 512 + 512)
+            dg = nt(DY[i], WD[l, j, cols, :])
+            dz = (GP[l, i, :, n * 512 : n * 512 + 512].astype(F32) * dg).astype(BF16)
+            term = nt(dz, WU[l, j, :, cols])
+            if n == 0:
+                ACC[...] = term
+            else:
+                ACC[...] += term
+
+        x_copy(1, i).wait_send()
+        SND[1, i] = ACC[...].astype(BF16)
+        x_copy(1, i).start()
+
+    def dr_copy(k, b):
+        rows = pl.ds(pl.multiple_of(b * R, R), R)
+        return pltpu.make_async_remote_copy(
+            DKV.at[:, rows, :], DR.at[k], dr_snd.at[k], dr_rcv.at[k], device_id=sib, device_id_type=MESH)
+
+    def attend_back(l, i):
+        b = blk_of(i)
+
+        def pair_turn(pair, carry):
+            lanes = head_lanes(pair)
+            qs = split_pair(Q[l, i, :, lanes], 1)
+            dos = split_pair(DO[:, lanes], 1)
+            rows_pair = pl.ds(pl.multiple_of(pair * 128, 128), 128)
+            dot_pair = DOT[rows_pair, :]
+            dots = split_pair(dot_pair, 0)
+            prod = dot_pair.astype(F32) * OT[l, i, rows_pair, :].astype(F32)
+            deltas = (
+                jnp.sum(prod[0:64], axis=0, keepdims=True),
+                jnp.sum(prod[64:128], axis=0, keepdims=True),
+            )
+            lses = (LSE[l, i, pair * 2], LSE[l, i, pair * 2 + 1])
+            OACC[...] = jnp.zeros(OACC.shape, F32)
+
+            def turn(j, c):
+                rows = pl.ds(pl.multiple_of(j * R, R), R)
+                keys = KV[l, 0, rows, lanes]
+                values = KV[l, 1, rows, lanes]
+                mask = MSK[i, rows, :].astype(F32)
+                dk = jnp.zeros((R, 128), F32)
+                dv = jnp.zeros((R, 128), F32)
+                for e in range(2):
+                    p = jnp.exp(nt(keys, qs[e]) + mask - lses[e])
+                    dp = nn(values, dots[e])
+                    ds = (p * (dp - deltas[e])).astype(BF16)
+                    dv += nn(p.astype(BF16), dos[e])
+                    dk += nn(ds, qs[e])
+                    OACC[e] += tn(keys, ds)
+                DKV[0, rows, lanes] += dk
+                DKV[1, rows, lanes] += dv
+                return c
+
+            lax.fori_loop(0, b + 1, turn, 0)
+            upper = lax.broadcasted_iota(jnp.int32, (128, R), 0) < HEAD_DIM
+            dq = jnp.where(upper, OACC[0], OACC[1]) * HEAD_DIM ** -0.5
+            DQ[pair // 2, :, pl.ds(pl.multiple_of((pair % 2) * 128, 128), 128)] = jnp.transpose(dq).astype(BF16)
+            return carry
+
+        lax.fori_loop(0, Q.shape[3] // 128, pair_turn, 0)
+
+    def backward_attention(l, i):
+        b = blk_of(i)
+        x_copy(1, i).wait_recv()
+
+        def rows_mid(rows):
+            g = swapped(1, i, rows) * vec(l, 2)
+            dmid = DY[i, rows, :].astype(F32) + norm_pull(MID[l, i, rows, :], g)
+            MID[l, i, rows, :] = dmid
+            AB[rows, :] = dmid.astype(BF16)
+
+        by_rows(rows_mid)
+        for j in range(2):
+            DOT[j * 256 : j * 256 + 256, :] = nt(WO[l, j], AB[...]).astype(BF16)
+            DO[:, j * 256 : j * 256 + 256] = nt(AB[...], WO[l, j]).astype(BF16)
+
+        @pl.when(i == 1)
+        def _():
+            @pl.when(l == 0)
+            def _():
+                @pl.when(s == 0)
+                def _():
+                    dr_copy(0, 1).wait_send()
+                    dr_copy(1, 2).wait_send()
+
+                @pl.when(s == 1)
+                def _():
+                    dr_copy(0, 0).wait_send()
+
+            def clear(r, c):
+                rows = pl.ds(pl.multiple_of(r * CHUNK, CHUNK), CHUNK)
+                DKV[:, rows, :] = jnp.zeros((2, CHUNK, DKV.shape[2]), F32)
+                return c
+
+            lax.fori_loop(0, 4 * R // CHUNK, clear, 0)
+
+        attend_back(l, i)
+        own = pl.ds(pl.multiple_of(b * R, R), R)
+
+        @pl.when((s == 0) & (i == 1))
+        def _():
+            dr_copy(0, 1).start()
+            dr_copy(1, 2).start()
+
+        @pl.when(b != 3)
+        def _():
+            def add(k):
+                dr_copy(k, b).wait_recv()
+                DKV[0, own, :] += DR[k, 0]
+                DKV[1, own, :] += DR[k, 1]
+
+            @pl.when(s == 1)
+            def _():
+                add(i)
+
+            @pl.when((s == 1) & (i == 0))
+            def _():
+                dr_copy(0, 0).start()
+
+            @pl.when(s == 0)
+            def _():
+                add(0)
+
+        for j in range(2):
+            cols = slice(j * 256, j * 256 + 256)
+            DQ[j, :, 256:512] = DKV[0, own, cols].astype(BF16)
+            DQ[j, :, 512:768] = DKV[1, own, cols].astype(BF16)
+
+        def rows_norm(rows):
+            xhat, _ = normalize(H[l, i, rows, :].astype(F32))
+            AB[rows, :] = (xhat * vec(l, 0) + vec(l, 1)).astype(BF16)
+
+        by_rows(rows_norm)
+        ups = [SP[l, j, 24:32, 0:768].astype(BF16) for j in range(2)]
+        du = (adapter_scale * (nt(DQ[0], ups[0]) + nt(DQ[1], ups[1]))).astype(BF16)
+        ga[l] += tn(du, AB[...])
+        for j in range(2):
+            gb[l, j] += adapter_scale * tn(U[l, i], DQ[j])
+
+        x_copy(0, i).wait_send()
+        SND[0, i] = (
+            nt(DQ[0], WQ[l, 0]) + nt(DQ[1], WQ[l, 1]) + nn(du, SP[l, 0, 8:16, :].astype(BF16))
+        ).astype(BF16)
+
+        @pl.when((l == 1) | (i != own_i))
+        def _():
+            x_copy(0, i).start()
+
+    def bwd_layer(back, carry):
+        l = 1 - back
+
+        def f_turn(k, c):
+            backward_ff(l, 1 - k)
+            return c
+
+        def a_turn(k, c):
+            backward_attention(l, 1 - k)
+            return c
+
+        lax.fori_loop(0, 2, f_turn, 0)
+
+        @pl.when(l == 1)
+        def _():
+            finish_forward()
+
+        lax.fori_loop(0, 2, a_turn, 0)
+        return carry
+
+    lax.fori_loop(0, 2, bwd_layer, 0)
+
+    x_copy(0, own_i).wait_recv()
+
+    def rows_out(rows):
+        g = swapped(0, own_i, rows) * vec(0, 0)
+        AB[rows, :] = (MID[0, own_i, rows, :] + norm_pull(H[0, own_i, rows, :].astype(F32), g)).astype(BF16)
+
+    by_rows(rows_out)
+    send_result(3, 0, AB)
+
+    x_copy(0, 1 - own_i).wait_send()
+    for i in range(2):
+        x_copy(1, i).wait_send()
+    x_copy(2, 1 - own_i).wait_send()
+    for p in range(5):
+        w_sib(p).wait_send()
+        w_y(p).wait_send()
+        w_forward(p).wait_send()
+    spread_done(tok, H.at[0], 0)
+    spread_done(cot, DY, 1)
+    for l in range(2):
+        kv_copy(l, 0).wait_send()
+
+        @pl.when(s == 1)
+        def _():
+            kv_copy(l, 1).wait_send()
+
+    @pl.when(s == 0)
+    def _():
+        dr_copy(0, 1).wait_send()
+        dr_copy(1, 2).wait_send()
+
+    @pl.when(s == 1)
+    def _():
+        dr_copy(0, 0).wait_send()
+
+    send_result_done(0, 0, H.at[1, 0])
+    send_result_done(1, 1, H.at[1, 0])
+    send_result_done(2, 1, H.at[1, 0])
+    send_result_done(3, 0, H.at[1, 0])
+    for o, ref in ((0, act), (1, ig)):
+        for m in range(2):
+            pltpu.make_async_copy(tok.at[0], ref.at[m], out_rcv.at[o, m]).wait()
+
+
+def per_pair(
+    tokens, cotangent, buckets, lengths, norm_gain_pairs, norm_bias_pairs, query_key_value_weight,
+    query_value_bias, output_weight, upward_weight, upward_bias, down_weight, output_bias,
+    adapter_down, adapter_upper,
+):
+    gains, shifts, biases = norm_gain_pairs[0], norm_bias_pairs[0], output_bias[0]
+    vectors = jnp.stack([gains[0], shifts[0], gains[1], shifts[1], biases[0], biases[1]])
+    bias_qv = query_value_bias[0]
+    width = bias_qv.shape[1]
+    upper = adapter_upper[0]
+    rank = upper.shape[1]
+    empty = jnp.zeros((1, width), BF16)
+    qkv_bias = jnp.concatenate([bias_qv[0:1], empty, bias_qv[1:2], empty], axis=1)
+    none = jnp.zeros((rank, width), BF16)
+    upper_rows = jnp.concatenate(
+        [
+            jnp.concatenate([upper[0], none, none, none], axis=1),
+            jnp.concatenate([none, none, upper[1], none], axis=1),
+        ]
+    )
+    down_rows = adapter_down[0].reshape(2 * rank, D)
+    small = jnp.concatenate(
+        [
+            vectors,
+            jnp.zeros((2, D), BF16),
+            down_rows,
+            upward_bias[0][None],
+            qkv_bias,
+            jnp.zeros((6, D), BF16),
+            upper_rows,
+        ]
+    ).astype(F32)
+    weight_qkv = query_key_value_weight[0].reshape(D, 3 * width)
+    anywhere = pl.BlockSpec(memory_space=pl.ANY)
+    scalars = pl.BlockSpec(memory_space=pltpu.SMEM)
+    vmem = pl.BlockSpec(memory_space=pltpu.VMEM)
+    dma = pltpu.SemaphoreType.DMA
+    act, ig, ga, gb = pl.pallas_call(
+        fused_kernel,
+        out_shape=(
+            jax.ShapeDtypeStruct((2, R, D), BF16),
+            jax.ShapeDtypeStruct((2, R, D), BF16),
+            jax.ShapeDtypeStruct((2, 8, D), F32),
+            jax.ShapeDtypeStruct((2, 2, 8, 768), F32),
+        ),
+        in_specs=[anywhere, anywhere, scalars, scalars] + [anywhere] * 5,
+        out_specs=(anywhere, anywhere, vmem, vmem),
+        scratch_shapes=[
+            pltpu.VMEM((2, 2, 32, D), F32),
+            pltpu.VMEM((2, 2, D, 768), BF16),
+            pltpu.VMEM((2, 2, 256, D), BF16),
+            pltpu.VMEM((2, 2, D, 1024), BF16),
+            pltpu.VMEM((2, 2, 1024, D), BF16),
+            pltpu.VMEM((2, 2, R, D), BF16),
+            pltpu.VMEM((2, R, D), BF16),
+            pltpu.VMEM((2, 2, R, D), F32),
+            pltpu.VMEM((2, 2, R, 2048), BF16),
+            pltpu.VMEM((2, 2, R, 512), BF16),
+            pltpu.VMEM((2, 2, 4 * R, 512), BF16),
+            pltpu.VMEM((2, 2, 512, R), BF16),
+            pltpu.VMEM((2, 2, 8, 1, R), F32),
+            pltpu.VMEM((3, 2, R, D), BF16),
+            pltpu.VMEM((3, 2, R, D), BF16),
+            pltpu.VMEM((R, D), F32),
+            pltpu.VMEM((2, 4 * R, R), F32),
+            pltpu.VMEM((2, 4 * R, R), BF16),
+            pltpu.VMEM((2, 4 * R, 512), F32),
+            pltpu.VMEM((2, 2, R, 512), F32),
+            pltpu.VMEM((2, R, 768), BF16),
+            pltpu.VMEM((512, R), BF16),
+            pltpu.VMEM((R, 512), BF16),
+            pltpu.VMEM((R, D), BF16),
+            pltpu.VMEM((2, 2, R, 8), BF16),
+            pltpu.VMEM((2, 128, R), F32),
+            dma((2, 2)),
+            dma((2, 3)),
+            dma((2, 2, 5)),
+            dma((5,)),
+            dma((5,)),
+            dma((5,)),
+            dma((5,)),
+            dma((2, 2)),
+            dma((2, 2)),
+            dma((3, 2)),
+            dma((3, 2)),
+            dma((2,)),
+            dma((2,)),
+            dma((2, 2)),
+            dma((4,)),
+        ],
+        compiler_params=pltpu.CompilerParams(
+            collective_id=0, has_side_effects=True, vmem_limit_bytes=63 * 2**20
+        ),
+        name="two_layers",
+    )(
+        tokens, cotangent, buckets, lengths, small, weight_qkv, output_weight[0],
+        upward_weight[0], down_weight[0],
+    )
+    s = lax.axis_index("section")
+    t = lax.axis_index("tensor")
+    part = jnp.stack([gb[:, :, 0:rank, 0:width], gb[:, :, rank : 2 * rank, 2 * width : 3 * width]], axis=1)
+    x = t % 2
+    zero = jnp.zeros_like(part)
+    both = jnp.where(x == 0, jnp.stack([part, zero], axis=3), jnp.stack([zero, part], axis=3))
+    wide = both.transpose(0, 1, 4, 2, 3, 5).reshape(2, 2, rank, 4 * width)
+    sums = lax.psum(jnp.stack([ga.reshape(2, 2, rank, D), wide]), ("section", "dp", "tensor"))
+    mine = lax.dynamic_index_in_dim(sums, s, 1, keepdims=False)
+    total_b = lax.dynamic_slice_in_dim(mine[1], t * width, width, 2)
+    return act[None], ig[None], mine[0][None], total_b[None]
+
+
 def solution(mesh):
     in_specs = (
         P("dp", "tensor", None),
@@ -368,6 +1154,7 @@
         P("section", None, None, None),
         P("section", None, None, "tensor"),
     )
+    pairs = mesh.shape["section"] == 2 and mesh.shape["tensor"] == 4
     return jax.shard_map(
-        per_device, mesh=mesh, in_specs=in_specs, out_specs=out_specs, check_vma=False
+        per_pair if pairs else per_device, mesh=mesh, in_specs=in_specs, out_specs=out_specs, check_vma=False
     )

time: 2430 us -> 476 us (0.20)
  waiting for transfers between devices: 1480 us -> 127 us
  matrix products: 524 us -> 0 us
  Pallas kernels: 0 us -> 319 us
  other arithmetic: 162 us -> 1.4 us
  blocking collectives: 85.5 us -> 0 us
  local copies, waits for them, and re-layouts: 88.5 us -> 14.5 us
  loops' own time: 52.2 us -> 0 us
    all_gather x24 -> x0, waiting for transfers between devices: 802 us -> none  [the longest x16 534 us: widen(): return lax.all_gather(values, 'tensor', axis=0, tiled=True)]
    reduce_scatter x20 -> x0, waiting for transfers between devices: 676 us -> none  [the longest x12 415 us: settle(): lax.psum_scatter(row_term(jnp.int32(0), lax.axis_size('tensor') * own_row...]
    dot_general x104 -> x0, matrix products: 435 us -> none  [the longest x12 61.3 us: row_term(): return jnp.dot(source, weight, preferred_element_type=jnp.float32)]
    pallas_call x0 -> x1, Pallas kernels: none -> 319 us  [per_pair(): pl.pallas_call(fused_kernel, out_shape=(jax.ShapeDtypeStruct((2, R, D), B...]
    psum x0 -> x1, waiting for transfers between devices: none -> 127 us  [per_pair(): lax.psum(jnp.stack([ga.reshape(2, 2, rank, D), wide]), ('section', 'dp',...]
    sub x8 -> x0, matrix products: 88.6 us -> none  [attend(): exponent = jnp.exp(scores - top_score)]
    psum x2 -> x0, blocking collectives: 85.5 us -> none  [the longest x1 76.4 us: per_device(): total_a = lax.psum(sum_a, ('dp', 'tensor'))]
    convert_element_type x33 -> x1, other arithmetic: 68.5 us -> 0.67 us  [per_pair(): small = jnp.concatenate([vectors, jnp.zeros((2, D), BF16), down_rows, upw...]
  transfers between devices with their start and end apart: 46 -> 1, of which waited for: 46 -> 1; matrix products, arithmetic and copies ran while one was open for 4% -> 0% of each run, Pallas kernels for 0% -> 0%
where the time goes in v1:
time: 476 us
  Pallas kernels  319 us (67%)
  waiting for transfers between devices  127 us (27%)
  local copies, waits for them, and re-layouts  14.5 us (3%)
  between operations  14.2 us (3%)
    pallas_call x1, Pallas kernels, per_pair(): pl.pallas_call(fused_kernel, out_shape=(jax.ShapeDtypeStruct((2, R, D), B...  319 us
    psum x1, waiting for transfers between devices, per_pair(): lax.psum(jnp.stack([ga.reshape(2, 2, rank, D), wide]), ('section', 'dp',...  127 us
  transfers between devices with their start and end apart: 1, of which 1 were waited for; matrix products, arithmetic and copies ran while one was open for 0% of the time, Pallas kernels for 0%

profile of v1, /device:TPU:0, one launch (start us, length us, event | category | flops | bytes accessed | tf_op | source)
XLA Modules:
  0.0 475.8 jit_solution(14025894728195653267)
XLA Ops:
  7.2 0.0 all-reduce.5.cloned.1.call-start
  7.2 0.8 slice_bitcast_fusion.5
  8.0 0.7 reshape_squeeze.6
  8.7 0.8 slice_bitcast_fusion.11
  9.5 0.7 slice_bitcast_fusion.8
  10.2 0.8 slice_bitcast_fusion.2
  11.1 0.8 concatenate.20
  11.9 0.7 convert_element_type.3.small_in
  12.6 1.7 copy.20
  14.3 1.6 copy.21.wq_in
  15.9 319.0 %two_layers.1 = (bf16[2,256,1024]{2,1,0:T(8,128)(2,1)}, bf16[2,256,1024]{2,1,0:T(8,128)(2,1)}, f32[2,8,1024]{2,1,0:T(8,128)}, f32[2,2,8,768]{3,2,1,0:T(8,128)}) custom-call(bf16[2,256,1024]{2,1,0:T(8,128)(2,1)} %tok.1, bf16[2,256,1024]{2,1,0:T(8,128)(2,1)} %cot.1, s32[2]{0:T(128)} %buckets.1, s32[2,8]{1,0:T(2,128)} %lengths.1, ...), custom_call_target="tpu_custom_call" | custom-call | tf_op jit(solution)/shard_map/two_layers/pallas_call | solution.py:1059
  334.9 0.0 copy-start.1
  334.9 0.9 slice_bitcast_fusion.1
  335.8 0.1 copy.22
  335.9 0.1 stack_reshape.7
  336.0 1.0 stack_reshape.6
  336.9 0.7 pad_maximum_fusion
  337.6 0.0 all-reduce.5.cloned.1.call-update
  337.7 126.7 %all-reduce.5.cloned.1.call-done = f32[2,2,2,4,1024]{4,3,2,1,0:T(4,128)} async-done(((f32[2,2,2,4,1024]{4,3,2,1,0:T(4,128)}), f32[2,2,2,4,1024]{4,3,2,1,0:T(4,128)}) %all-reduce.5.cloned.1.call-update) | async-done | bytes 131088 | tf_op jit(solution)/shard_map/psum | solution.py:1127
  464.4 1.4 dynamic-slice_bitcast_fusion
  465.7 1.3 dynamic-slice_bitcast_fusion.1
  467.0 0.0 copy-done.1
  467.0 1.0 copy.26
  468.0 1.0 copy.27
  (14 shorter events, 0.1 us)
Async XLA Ops:
  7.2 457.2 %all-reduce.5.cloned.1.call-start = ((), (), s32[]{:S(2)}) async-start(), calls=%async_computation | async-start | bytes 262144 | tf_op jit(solution)/shard_map/psum | solution.py:1127
  334.9 132.1 %copy-start.1 = (bf16[2,256,1024]{2,1,0:T(8,128)(2,1)S(1)}, bf16[2,256,1024]{2,1,0:T(8,128)(2,1)}, u32[]{:S(2)}) copy-start(bf16[2,256,1024]{2,1,0:T(8,128)(2,1)} %get-tuple-element.8) | copy-start | bytes 3145732
  335.8 132.2 %copy-start = (bf16[2,256,1024]{2,1,0:T(8,128)(2,1)S(1)}, bf16[2,256,1024]{2,1,0:T(8,128)(2,1)}, u32[]{:S(2)}) copy-start(bf16[2,256,1024]{2,1,0:T(8,128)(2,1)} %get-tuple-element.9) | copy-start | bytes 3145732
Sparse Core Ops, SparseCore 0:
  337.8 126.5 all-reduce.4

commit v2 on v1

--- a/solution.py
+++ b/solution.py
@@ -352,7 +352,7 @@
 F32 = jnp.float32
 BF16 = jnp.bfloat16
 MESH = pl.DeviceIdType.MESH
-CHUNK = 32
+CHUNK = 128
 
 
 def nn(a, b):
@@ -392,12 +392,13 @@
 
 
 def fused_kernel(
-    tok, cot, buckets, lengths, small_in, wq_in, wo_in, wu_in, wd_in,
-    act, ig, ga, gb,
-    SP, WQ, WO, WU, WD, H, DY, MID, GP, Q, KV, OT, LSE, SND, RCV, ACC, ST, MSK,
-    DKV, DR, DQ, DOT, DO, AB, U, OACC,
-    tok_sem, tok_snd, wsem, wloc, wsib, wy, wfwd, kv_rcv, kv_snd, x_rcv, x_snd,
-    dr_rcv, dr_snd, out_rcv, out_snd,
+    dp_count,
+    tok, cot, buckets, lengths, gain_in, shift_in, wq_in, bqv_in, wo_in, wu_in, bu_in, wd_in, bo_in, ad_in, au_in,
+    act, ig, out_a, out_b,
+    SP, WQ, WO, WU, WD, H, DY, MID, GP, Q, KV, OT, LSE, SND, RCV, BIG, MSK, DR, DQ, AB, U, OACC, PB,
+    GA, GB, GCA, GCB, GXA, GXB, GZA, GZB,
+    tok_sem, tok_ys, tok_xs, wl, ws_r, ws_s, wy_r, wy_s, wz_r, wz_s, wa_r, wa_s, wb_r, wb_s,
+    kv_rcv, kv_snd, x_rcv, x_snd, dr_rcv, dr_snd, out_rcv, out_snd, gc_r, gc_s, gx_r, gx_s, gz_r, gz_s,
 ):
     s = lax.axis_index("section")
     d = lax.axis_index("dp")
@@ -407,6 +408,8 @@
     sib = (1 - s, d, t)
     xp = (s, d, y * 2 + 1 - x)
     yp = (s, d, (1 - y) * 2 + x)
+    z_half = lax.rem(d, 2)
+    zp = (s, d + 1 - 2 * z_half, t)
     flip = s + x - 2 * s * x
     own_i = flip
 
@@ -422,82 +425,172 @@
                     x2 = 1 - x if dx else x
                     y2 = 1 - y if dy else y
                     pl.semaphore_signal(bar, 1, device_id=(s2, d, y2 * 2 + x2), device_id_type=MESH)
-    pl.semaphore_wait(bar, 7)
-
-    my_core = x + y - 2 * x * y
-
-    def spread(src, dst, which):
-        @pl.when(s == my_core)
-        def _():
-            for k, (dx, dy) in enumerate(((1, 0), (0, 1), (1, 1))):
-                x2 = 1 - x if dx else x
-                y2 = 1 - y if dy else y
+    for k in range(1, dp_count):
+        pl.semaphore_signal(bar, 1, device_id=(s, lax.rem(d + k, dp_count), t), device_id_type=MESH)
+    pl.semaphore_wait(bar, 7 + dp_count - 1)
+
+    def row_copies(src, dst, w):
+        def local():
+            return pltpu.make_async_copy(src.at[y], dst.at[y], tok_sem.at[w, y])
+
+        def to_y():
+            return pltpu.make_async_remote_copy(
+                src.at[1 - y], dst.at[y], tok_ys.at[w], tok_sem.at[w, y], device_id=yp, device_id_type=MESH)
+
+        def first_x():
+            return pltpu.make_async_remote_copy(
+                src.at[y], dst.at[y], tok_xs.at[w], tok_sem.at[w, y], device_id=xp, device_id_type=MESH)
+
+        def then_x():
+            return pltpu.make_async_remote_copy(
+                dst.at[own_i], dst.at[own_i], tok_xs.at[w], tok_sem.at[w, own_i],
+                device_id=xp, device_id_type=MESH)
+
+        return local, to_y, first_x, then_x
+
+    def rows_start(src, dst, w):
+        local, to_y, first_x, _ = row_copies(src, dst, w)
+
+        @pl.when(y == own_i)
+        def _():
+            first_x().start()
+            to_y().start()
+            local().start()
+
+    def rows_relay(src, dst, w):
+        pltpu.make_async_copy(src.at[0], dst.at[own_i], tok_sem.at[w, own_i]).wait()
+
+        @pl.when(y != own_i)
+        def _():
+            row_copies(src, dst, w)[3]().start()
+
+    def rows_rest(src, dst, w):
+        pltpu.make_async_copy(src.at[0], dst.at[1 - own_i], tok_sem.at[w, 1 - own_i]).wait()
+
+    def rows_done(src, dst, w):
+        _, to_y, first_x, _ = row_copies(src, dst, w)
+        if w == 0:
+            first_x().wait_send()
+
+        @pl.when(y == own_i)
+        def _():
+            to_y().wait_send()
+
+    pieces = (None, (wq_in, WQ, 2), (wo_in, WO, 1), (wu_in, WU, 2), (wd_in, WD, 2))
+    base = (7, 0, 2, 3, 5)
+
+    def sources(p, rows):
+        src, dst, _ = pieces[p]
+        if p == 1:
+            return [
+                (src.at[c, rows, :], dst.at[s, y, rows, c * 256 : c * 256 + 256]) for c in range(3)
+            ]
+        return [(src.at[0, rows, :], dst.at[s, y, rows, :])]
+
+    def chunk(p, c, half):
+        dst, parts = pieces[p][1], pieces[p][2]
+        size = dst.shape[2] // (2 * parts)
+        return pl.ds(pl.multiple_of((half * parts + c) * size, size), size)
+
+    def block(p, l, j, rows):
+        return pieces[p][1].at[l, j, rows, :]
+
+    def own_start(p):
+        everything = pl.ds(0, pieces[p][1].shape[2])
+        for src, dst in sources(p, everything):
+            pltpu.make_async_copy(src, dst, wl.at[p]).start()
+            pltpu.make_async_remote_copy(
+                src, dst, ws_s.at[p], ws_r.at[p], device_id=sib, device_id_type=MESH).start()
+
+    def y_start(p):
+        if p == 0:
+            small_copy(yp, wy_s.at[7], wy_r.at[7]).start()
+            return
+        for c in range(pieces[p][2]):
+            for src, dst in sources(p, chunk(p, c, z_half)):
+                k = base[p] + c
                 pltpu.make_async_remote_copy(
-                    src.at[y2], dst.at[y], tok_snd.at[which, k], tok_sem.at[which, y],
-                    device_id=(s, d, y2 * 2 + x2), device_id_type=MESH,
-                ).start()
-            pltpu.make_async_copy(src.at[y], dst.at[y], tok_sem.at[which, y]).start()
-
-    def spread_done(src, dst, which):
-        @pl.when(s == my_core)
-        def _():
-            for k, (dx, dy) in enumerate(((1, 0), (0, 1), (1, 1))):
-                x2 = 1 - x if dx else x
-                y2 = 1 - y if dy else y
-                pltpu.make_async_remote_copy(
-                    src.at[y2], dst.at[y], tok_snd.at[which, k], tok_sem.at[which, y],
-                    device_id=(s, d, y2 * 2 + x2), device_id_type=MESH,
-                ).wait_send()
-
-    pieces = ((small_in, SP), (wq_in, WQ), (wo_in, WO), (wu_in, WU), (wd_in, WD))
-
-    def w_local(p):
-        src, dst = pieces[p]
-        return pltpu.make_async_copy(src, dst.at[s, y], wsem.at[s, y, p])
-
-    def w_sib(p):
-        src, dst = pieces[p]
+                    src, dst, wy_s.at[k], wy_r.at[k], device_id=yp, device_id_type=MESH).start()
+
+    def small_copy(to, snd, rcv):
         return pltpu.make_async_remote_copy(
-            src, dst.at[s, y], wsib.at[p], wsem.at[s, y, p], device_id=sib, device_id_type=MESH)
-
-    def w_y(p):
-        src, dst = pieces[p]
-        return pltpu.make_async_remote_copy(
-            src, dst.at[s, y], wy.at[p], wsem.at[s, y, p], device_id=yp, device_id_type=MESH)
-
-    def w_forward(p):
-        dst = pieces[p][1]
-        return pltpu.make_async_remote_copy(
-            dst.at[s, 1 - y], dst.at[s, 1 - y], wfwd.at[p], wsem.at[s, 1 - y, p],
-            device_id=sib, device_id_type=MESH)
-
-    def w_wait(l, j, p):
-        src, dst = pieces[p]
-        pltpu.make_async_copy(src, dst.at[l, j], wsem.at[l, j, p]).wait()
-
-    def w_ready(l, p):
-        w_wait(l, 0, p)
-        w_wait(l, 1, p)
+            SP.at[s, y], SP.at[s, y], snd, rcv, device_id=to, device_id_type=MESH)
+
+    def passed(p, c, half, to, snd, rcv):
+        ref = SP.at[s, 1 - y] if p == 0 else block(p, s, 1 - y, chunk(p, c, half))
+        return pltpu.make_async_remote_copy(ref, ref, snd, rcv, device_id=to, device_id_type=MESH)
+
+    def relay_y(l, p, c=0):
+        k = base[p] + c
 
         @pl.when(l == s)
         def _():
-            w_forward(p).start()
-
-    spread(tok, H.at[0], 0)
-    for p in range(2):
-        w_local(p).start()
-        w_sib(p).start()
-
-        @pl.when(s == 0)
-        def _():
-            w_y(p).start()
-    for p in range(2, 5):
-        w_local(p).start()
-        w_sib(p).start()
-
-        @pl.when(s == 0)
-        def _():
-            w_y(p).start()
+            passed(p, c, z_half, sib, wa_s.at[k], wy_r.at[k]).wait_recv()
+            if p:
+                passed(p, c, z_half, zp, wz_s.at[k], wz_r.at[k]).start()
+            passed(p, c, z_half, sib, wa_s.at[k], wa_r.at[k]).start()
+
+    def relay_z(l, p, c=0):
+        k = base[p] + c
+
+        @pl.when(l == s)
+        def _():
+            passed(p, c, 1 - z_half, zp, wz_s.at[k], wz_r.at[k]).wait_recv()
+            passed(p, c, 1 - z_half, sib, wb_s.at[k], wb_r.at[k]).start()
+
+    def own_wait(l, p):
+        @pl.when(l == s)
+        def _():
+            if p:
+                ref = pieces[p][1].at[s, y]
+                pltpu.make_async_copy(ref, ref, wl.at[p]).wait()
+
+        @pl.when(l != s)
+        def _():
+            ref = pieces[p][1].at[1 - s, y] if p else SP.at[1 - s, y]
+            pltpu.make_async_copy(ref, ref, ws_r.at[p]).wait()
+
+    def other_wait(l, p):
+        @pl.when(l != s)
+        def _():
+            if p == 0:
+                ref = SP.at[1 - s, 1 - y]
+                pltpu.make_async_copy(ref, ref, wa_r.at[7]).wait()
+            else:
+                for c in range(pieces[p][2]):
+                    k = base[p] + c
+                    ref = block(p, 1 - s, 1 - y, chunk(p, c, 0))
+                    pltpu.make_async_copy(ref, ref, wa_r.at[k]).wait()
+                    pltpu.make_async_copy(ref, ref, wb_r.at[k]).wait()
+
+    @pl.when(s == 0)
+    def _():
+        y_start(1)
+
+    rows_start(tok, H.at[0], 0)
+    SP[s, y] = jnp.zeros(SP.shape[2:], F32)
+    for k, (ref, row) in enumerate(
+        ((gain_in, 0), (shift_in, 0), (gain_in, 1), (shift_in, 1), (bo_in, 0), (bo_in, 1))
+    ):
+        SP[s, y, k : k + 1, :] = ref[0, row : row + 1, :].astype(F32)
+    SP[s, y, 8:12, :] = ad_in[0, 0].astype(F32)
+    SP[s, y, 12:16, :] = ad_in[0, 1].astype(F32)
+    SP[s, y, 16:17, :] = bu_in[...].astype(F32)
+    SP[s, y, 17:18, 0:256] = bqv_in[0, 0:1, :].astype(F32)
+    SP[s, y, 17:18, 512:768] = bqv_in[0, 1:2, :].astype(F32)
+    SP[s, y, 24:28, 0:256] = au_in[0, 0].astype(F32)
+    SP[s, y, 28:32, 512:768] = au_in[0, 1].astype(F32)
+    small_copy(sib, ws_s.at[0], ws_r.at[0]).start()
+    for p in range(1, 5):
+        own_start(p)
+
+    @pl.when(s == 0)
+    def _():
+        y_start(0)
+        for p in range(2, 5):
+            y_start(p)
+
+    rows_start(cot, DY, 1)
 
     shift = 7 + buckets[y]
     span_mask = lax.shift_left(jnp.int32(1), shift) - 1
@@ -521,30 +614,36 @@
             k_tag = jnp.where(k_ok, k_item, -1)
             same = (k_tag == q_item) & (k_row <= q_row)
             allowed = same | (k_row == q_row)
-            MSK[i, pl.ds(r0, CHUNK), :] = jnp.where(allowed, 0.0, NEG).astype(BF16)
+            MSK[pl.ds(pl.multiple_of(i * 2 * R + r0, CHUNK), CHUNK), :] = jnp.where(allowed, 0.0, NEG).astype(BF16)
             return carry
 
         lax.fori_loop(0, (b + 1) * (R // CHUNK), rows, 0)
 
     build_mask(0)
     build_mask(1)
-    ga[...] = jnp.zeros(ga.shape, F32)
-    gb[...] = jnp.zeros(gb.shape, F32)
+    GA[...] = jnp.zeros(GA.shape, F32)
+    GB[...] = jnp.zeros(GB.shape, F32)
 
     def x_copy(slot, i):
         return pltpu.make_async_remote_copy(
-            SND.at[slot, i], RCV.at[slot, i], x_snd.at[slot, i], x_rcv.at[slot, i],
+            SND.at[slot, i], RCV.at[slot * 2 + (i if slot < 2 else 0)], x_snd.at[slot, i], x_rcv.at[slot, i],
             device_id=xp, device_id_type=MESH)
 
-    def by_rows(body, step=CHUNK):
-        def turn(r, carry):
-            body(pl.ds(pl.multiple_of(r * step, step), step))
-            return carry
-
-        lax.fori_loop(0, R // step, turn, 0)
+    def by_rows(body):
+        body(slice(0, R))
+
+    total_rows = slice(3 * R, 4 * R)
+
+    def gather(n, term):
+        for c in range(4):
+            part = term[:, c * R : c * R + R]
+            BIG[c, total_rows, :] = part if n == 0 else BIG[c, total_rows, :] + part
+
+    def gathered():
+        return jnp.concatenate([BIG[c, total_rows, :] for c in range(4)], axis=1).astype(BF16)
 
     def swapped(slot, i, rows):
-        return SND[slot, i, rows, :].astype(F32) + RCV[slot, i, rows, :].astype(F32)
+        return SND[slot, i, rows, :].astype(F32) + RCV[slot * 2 + (i if slot < 2 else 0), rows, :].astype(F32)
 
     def send_result(which, layer, src):
         dst = act if which < 2 else ig
@@ -596,58 +695,85 @@
             KV.at[l, :, rows, :], KV.at[l, :, rows, :], kv_snd.at[l, i], kv_rcv.at[l, i],
             device_id=sib, device_id_type=MESH).wait_recv()
 
+    GROUP = 4
+
     def attend(l, i):
         b = blk_of(i)
 
-        def pair_turn(pair, carry):
-            lanes = head_lanes(pair)
-            qs = split_pair(Q[l, i, :, lanes], 1)
+        def group_turn(g, carry):
+            def lanes_of(k):
+                return pl.ds(pl.multiple_of(g * (GROUP * HEAD_DIM) + k * 128, 128), 128)
 
             def first(j, tops):
                 rows = pl.ds(pl.multiple_of(j * R, R), R)
-                keys = KV[l, 0, rows, lanes]
-                mask = MSK[i, rows, :].astype(F32)
+                mask = MSK[pl.ds(pl.multiple_of((i * 2 + j) * R, R), R), :].astype(F32)
                 new = []
-                for e in range(2):
-                    st = nt(keys, qs[e]) + mask
-                    ST[e, rows, :] = st
-                    new.append(jnp.maximum(tops[e], jnp.max(st, axis=0, keepdims=True)))
+                for k in range(GROUP // 2):
+                    qs = split_pair(Q[l, i, :, lanes_of(k)], 1)
+                    keys = KV[l, 0, rows, lanes_of(k)]
+                    for e in range(2):
+                        st = nt(keys, qs[e]) + mask
+                        BIG[2 * k + e, rows, :] = st
+                        new.append(jnp.maximum(tops[2 * k + e], jnp.max(st, axis=0, keepdims=True)))
                 return tuple(new)
 
-            tops = lax.fori_loop(0, b + 1, first, (jnp.full((1, R), NEG, F32),) * 2)
-            OACC[...] = jnp.zeros(OACC.shape, F32)
+            tops = lax.fori_loop(0, b + 1, first, (jnp.full((1, R), NEG, F32),) * GROUP)
+            for k in range(GROUP):
+                OACC[k] = jnp.zeros(OACC.shape[1:], F32)
 
             def second(j, sums):
                 rows = pl.ds(pl.multiple_of(j * R, R), R)
-                values = KV[l, 1, rows, lanes]
                 new = []
-                for e in range(2):
-                    p = jnp.exp(ST[e, rows, :] - tops[e])
-                    new.append(sums[e] + jnp.sum(p, axis=0, keepdims=True))
-                    OACC[e] += tn(values, p.astype(BF16))
+                for k in range(GROUP):
+                    p = jnp.exp(BIG[k, rows, :] - tops[k])
+                    new.append(sums[k] + jnp.sum(p, axis=0, keepdims=True))
+                    PB[k] = p.astype(BF16)
+                for k in range(GROUP // 2):
+                    values = jnp.transpose(KV[l, 1, rows, lanes_of(k)])
+                    for e in range(2):
+                        OACC[2 * k + e] += nn(values[e * 64 : e * 64 + 64], PB[2 * k + e])
                 return tuple(new)
 
-            sums = lax.fori_loop(0, b + 1, second, (jnp.zeros((1, R), F32),) * 2)
-            for e in range(2):
-                OT[l, i, pl.ds(pl.multiple_of(pair * 128 + e * 64, 64), 64), :] = (
-                    OACC[e, e * 64 : e * 64 + 64, :] * (1.0 / sums[e])
+            sums = lax.fori_loop(0, b + 1, second, (jnp.zeros((1, R), F32),) * GROUP)
+            for k in range(GROUP):
+                OT[l, i, pl.ds(pl.multiple_of((g * GROUP + k) * 64, 64), 64), :] = (
+                    OACC[k] * (1.0 / sums[k])
                 ).astype(BF16)
-                LSE[l, i, pair * 2 + e] = tops[e] + jnp.log(sums[e])
+                LSE[l, i, g * GROUP + k] = tops[k] + jnp.log(sums[k])
             return carry
 
-        lax.fori_loop(0, Q.shape[3] // 128, pair_turn, 0)
+        lax.fori_loop(0, Q.shape[3] // (GROUP * HEAD_DIM), group_turn, 0)
 
     def forward_attention(l, i):
         b = blk_of(i)
 
         @pl.when(i == 0)
         def _():
-            w_ready(l, 0)
-            w_ready(l, 1)
-
-        @pl.when(l == 0)
-        def _():
-            pltpu.make_async_copy(tok.at[0], H.at[0, i], tok_sem.at[0, i]).wait()
+            @pl.when(l == 0)
+            def _():
+                relay_y(l, 1, 0)
+                rows_relay(tok, H.at[0], 0)
+                relay_y(l, 0)
+                relay_y(l, 1, 1)
+                relay_z(l, 1, 0)
+                rows_rest(tok, H.at[0], 0)
+
+            own_wait(l, 0)
+            other_wait(l, 0)
+            own_wait(l, 1)
+
+            @pl.when(l == 1)
+            def _():
+                relay_z(l, 1, 0)
+
+            relay_y(l, 2)
+            relay_z(l, 1, 1)
+            other_wait(l, 1)
+
+        @pl.when(i == 1)
+        def _():
+            relay_y(l, 3, 0)
+            relay_y(l, 3, 1)
 
         @pl.when(l == 1)
         def _():
@@ -669,7 +795,7 @@
 
         by_rows(rows_norm)
         u = nt(AB[...], SP[l, 0, 8:16, :].astype(BF16)).astype(BF16)
-        U[l, i] = u
+        U[l, i] = nt(SP[l, 0, 8:16, :].astype(BF16), AB[...]).astype(BF16)
         own_rows = pl.ds(pl.multiple_of(b * R, R), R)
         for j in range(2):
             up = SP[l, j, 24:32, 0:768].astype(BF16)
@@ -696,7 +822,9 @@
 
         @pl.when(i == 0)
         def _():
-            w_ready(l, 2)
+            own_wait(l, 2)
+            relay_z(l, 2)
+            other_wait(l, 2)
 
         @pl.when(l == 1)
         def _():
@@ -711,10 +839,22 @@
             @pl.when((s == 1) & (l == 0))
             def _():
                 for p in range(5):
-                    w_y(p).start()
-
-            w_ready(l, 3)
-            w_ready(l, 4)
+                    y_start(p)
+
+            own_wait(l, 3)
+            own_wait(l, 4)
+            relay_z(l, 3, 0)
+            relay_y(l, 4, 0)
+            relay_z(l, 3, 1)
+            relay_y(l, 4, 1)
+
+        @pl.when((i == 1) & (l == 0))
+        def _():
+            rows_relay(cot, DY, 1)
+            rows_rest(cot, DY, 1)
+            relay_y(1, 0)
+            relay_y(1, 1, 0)
+            relay_y(1, 1, 1)
 
         x_copy(0, i).wait_recv()
 
@@ -726,18 +866,23 @@
 
         by_rows(rows_mid)
         for n in range(4):
-            j, half = n // 2, n % 2
+            j, half = (y if n < 2 else 1 - y), n % 2
             cols = slice(half * 512, half * 512 + 512)
+            if n == 2:
+
+                @pl.when(i == 0)
+                def _():
+                    relay_z(l, 4, 0)
+                    relay_z(l, 4, 1)
+                    other_wait(l, 3)
+                    other_wait(l, 4)
+
             z = nn(AB[...], WU[l, j, :, cols]) + SP[l, j, 16:17, cols]
             g, slope = gelu_pair(z)
             GP[l, i, :, n * 512 : n * 512 + 512] = slope.astype(BF16)
             term = nn(g.astype(BF16), WD[l, j, cols, :])
-            if n == 0:
-                ACC[...] = term
-            else:
-                ACC[...] += term
-        slot = 1 + l
-        SND[slot, i] = ACC[...].astype(BF16)
+            gather(n, term)
+        SND[1 + l, i] = gathered()
 
         @pl.when(l == 0)
         def _():
@@ -748,10 +893,6 @@
             x_copy(2, i).start()
 
     def fwd_layer(l, carry):
-        @pl.when(l == 1)
-        def _():
-            spread(cot, DY, 1)
-
         def a_turn(i, c):
             forward_attention(l, i)
             return c
@@ -779,10 +920,12 @@
     def backward_ff(l, i):
         @pl.when(l == 1)
         def _():
-            pltpu.make_async_copy(cot.at[0], DY.at[i], tok_sem.at[1, i]).wait()
+            @pl.when(i == own_i)
+            def _():
+                row_copies(cot, DY, 1)[3]().wait_send()
 
             def rows_valid(rows):
-                pos = blk_of(i) * R + rows.start + lax.broadcasted_iota(jnp.int32, (CHUNK, 1), 0)
+                pos = blk_of(i) * R + lax.broadcasted_iota(jnp.int32, (R, 1), 0)
                 _, ok = length_of(pos)
                 DY[i, rows, :] = (DY[i, rows, :].astype(F32) * jnp.where(ok, 1.0, 0.0)).astype(BF16)
 
@@ -803,68 +946,72 @@
                 send_result(2, 1, DY.at[i])
 
         for n in range(4):
-            j, half = n // 2, n % 2
+            j, half = (y if n < 2 else 1 - y), n % 2
             cols = slice(half * 512, half * 512 + 512)
             dg = nt(DY[i], WD[l, j, cols, :])
             dz = (GP[l, i, :, n * 512 : n * 512 + 512].astype(F32) * dg).astype(BF16)
             term = nt(dz, WU[l, j, :, cols])
-            if n == 0:
-                ACC[...] = term
-            else:
-                ACC[...] += term
+            gather(n, term)
 
         x_copy(1, i).wait_send()
-        SND[1, i] = ACC[...].astype(BF16)
+        SND[1, i] = gathered()
         x_copy(1, i).start()
 
     def dr_copy(k, b):
         rows = pl.ds(pl.multiple_of(b * R, R), R)
         return pltpu.make_async_remote_copy(
-            DKV.at[:, rows, :], DR.at[k], dr_snd.at[k], dr_rcv.at[k], device_id=sib, device_id_type=MESH)
+            BIG.at[:, rows, :], DR.at[k], dr_snd.at[k], dr_rcv.at[k], device_id=sib, device_id_type=MESH)
 
     def attend_back(l, i):
         b = blk_of(i)
-
-        def pair_turn(pair, carry):
-            lanes = head_lanes(pair)
-            qs = split_pair(Q[l, i, :, lanes], 1)
-            dos = split_pair(DO[:, lanes], 1)
-            rows_pair = pl.ds(pl.multiple_of(pair * 128, 128), 128)
-            dot_pair = DOT[rows_pair, :]
-            dots = split_pair(dot_pair, 0)
-            prod = dot_pair.astype(F32) * OT[l, i, rows_pair, :].astype(F32)
-            deltas = (
-                jnp.sum(prod[0:64], axis=0, keepdims=True),
-                jnp.sum(prod[64:128], axis=0, keepdims=True),
-            )
-            lses = (LSE[l, i, pair * 2], LSE[l, i, pair * 2 + 1])
-            OACC[...] = jnp.zeros(OACC.shape, F32)
-
-            def turn(j, c):
-                rows = pl.ds(pl.multiple_of(j * R, R), R)
+        pairs = Q.shape[3] // 128
+        place = RCV.at[2 + i]
+
+        def back_rows(k):
+            return place[(k % 2) * 128 : (k % 2) * 128 + 128, 512 + (k // 2) * 256 : 768 + (k // 2) * 256]
+
+        deltas = []
+        for k in range(pairs):
+            rows = slice(k * 128, k * 128 + 128)
+            prod = back_rows(k).astype(F32) * OT[l, i, rows, :].astype(F32)
+            deltas.append(jnp.sum(prod[0:64], axis=0, keepdims=True))
+            deltas.append(jnp.sum(prod[64:128], axis=0, keepdims=True))
+            OACC[2 * k] = jnp.zeros(OACC.shape[1:], F32)
+            OACC[2 * k + 1] = jnp.zeros(OACC.shape[1:], F32)
+
+        def turn(j, c):
+            rows = pl.ds(pl.multiple_of(j * R, R), R)
+            mask = MSK[pl.ds(pl.multiple_of((i * 2 + j) * R, R), R), :].astype(F32)
+            for k in range(pairs):
+                lanes = slice(k * 128, k * 128 + 128)
+                qs = split_pair(Q[l, i, :, lanes], 1)
+                dots = split_pair(back_rows(k), 0)
                 keys = KV[l, 0, rows, lanes]
                 values = KV[l, 1, rows, lanes]
-                mask = MSK[i, rows, :].astype(F32)
-                dk = jnp.zeros((R, 128), F32)
-                dv = jnp.zeros((R, 128), F32)
                 for e in range(2):
-                    p = jnp.exp(nt(keys, qs[e]) + mask - lses[e])
+                    h = 2 * k + e
+                    p = jnp.exp(nt(keys, qs[e]) + mask - LSE[l, i, h])
                     dp = nn(values, dots[e])
-                    ds = (p * (dp - deltas[e])).astype(BF16)
-                    dv += nn(p.astype(BF16), dos[e])
-                    dk += nn(ds, qs[e])
-                    OACC[e] += tn(keys, ds)
-                DKV[0, rows, lanes] += dk
-                DKV[1, rows, lanes] += dv
-                return c
-
-            lax.fori_loop(0, b + 1, turn, 0)
-            upper = lax.broadcasted_iota(jnp.int32, (128, R), 0) < HEAD_DIM
-            dq = jnp.where(upper, OACC[0], OACC[1]) * HEAD_DIM ** -0.5
-            DQ[pair // 2, :, pl.ds(pl.multiple_of((pair % 2) * 128, 128), 128)] = jnp.transpose(dq).astype(BF16)
-            return carry
-
-        lax.fori_loop(0, Q.shape[3] // 128, pair_turn, 0)
+                    PB[h] = (p * (dp - deltas[h])).astype(BF16)
+                    PB[2 * pairs + h] = p.astype(BF16)
+            for k in range(pairs):
+                lanes = slice(k * 128, k * 128 + 128)
+                half = slice((k % 2) * 128, (k % 2) * 128 + 128)
+                qs = split_pair(Q[l, i, :, lanes], 1)
+                dos = split_pair(place[:, lanes], 1)
+                h = 2 * k
+                BIG[k // 2, rows, half] += nn(PB[h], qs[0]) + nn(PB[h + 1], qs[1])
+                BIG[2 + k // 2, rows, half] += nn(PB[2 * pairs + h], dos[0]) + nn(PB[2 * pairs + h + 1], dos[1])
+            for k in range(pairs):
+                keys = jnp.transpose(KV[l, 0, rows, k * 128 : k * 128 + 128])
+                for e in range(2):
+                    OACC[2 * k + e] += nn(keys[e * 64 : e * 64 + 64], PB[2 * k + e])
+            return c
+
+        lax.fori_loop(0, b + 1, turn, 0)
+        for k in range(pairs):
+            dq = jnp.concatenate([OACC[2 * k], OACC[2 * k + 1]], axis=0) * HEAD_DIM ** -0.5
+            DQ[k // 2, :, (k % 2) * 128 : (k % 2) * 128 + 128] = jnp.transpose(dq).astype(BF16)
 
     def backward_attention(l, i):
         b = blk_of(i)
@@ -878,8 +1025,8 @@
 
         by_rows(rows_mid)
         for j in range(2):
-            DOT[j * 256 : j * 256 + 256, :] = nt(WO[l, j], AB[...]).astype(BF16)
-            DO[:, j * 256 : j * 256 + 256] = nt(AB[...], WO[l, j]).astype(BF16)
+            RCV[2 + i, :, 512 + j * 256 : 768 + j * 256] = nt(WO[l, j], AB[...]).astype(BF16)
+            RCV[2 + i, :, j * 256 : j * 256 + 256] = nt(AB[...], WO[l, j]).astype(BF16)
 
         @pl.when(i == 1)
         def _():
@@ -895,11 +1042,11 @@
                     dr_copy(0, 0).wait_send()
 
             def clear(r, c):
-                rows = pl.ds(pl.multiple_of(r * CHUNK, CHUNK), CHUNK)
-                DKV[:, rows, :] = jnp.zeros((2, CHUNK, DKV.shape[2]), F32)
+                rows = pl.ds(pl.multiple_of(r * R, R), R)
+                BIG[:, rows, :] = jnp.zeros((4, R, 256), F32)
                 return c
 
-            lax.fori_loop(0, 4 * R // CHUNK, clear, 0)
+            lax.fori_loop(0, 4, clear, 0)
 
         attend_back(l, i)
         own = pl.ds(pl.multiple_of(b * R, R), R)
@@ -913,8 +1060,8 @@
         def _():
             def add(k):
                 dr_copy(k, b).wait_recv()
-                DKV[0, own, :] += DR[k, 0]
-                DKV[1, own, :] += DR[k, 1]
+                for c in range(4):
+                    BIG[c, own, :] += DR[k, c]
 
             @pl.when(s == 1)
             def _():
@@ -929,9 +1076,8 @@
                 add(0)
 
         for j in range(2):
-            cols = slice(j * 256, j * 256 + 256)
-            DQ[j, :, 256:512] = DKV[0, own, cols].astype(BF16)
-            DQ[j, :, 512:768] = DKV[1, own, cols].astype(BF16)
+            DQ[j, :, 256:512] = BIG[j, own, :].astype(BF16)
+            DQ[j, :, 512:768] = BIG[2 + j, own, :].astype(BF16)
 
         def rows_norm(rows):
             xhat, _ = normalize(H[l, i, rows, :].astype(F32))
@@ -939,28 +1085,112 @@
 
         by_rows(rows_norm)
         ups = [SP[l, j, 24:32, 0:768].astype(BF16) for j in range(2)]
-        du = (adapter_scale * (nt(DQ[0], ups[0]) + nt(DQ[1], ups[1]))).astype(BF16)
-        ga[l] += tn(du, AB[...])
+        du = (adapter_scale * (nt(ups[0], DQ[0]) + nt(ups[1], DQ[1]))).astype(BF16)
+        GA[l] += nn(du, AB[...])
+        top = lax.broadcasted_iota(jnp.int32, (8, 256), 0) < 4
         for j in range(2):
-            gb[l, j] += adapter_scale * tn(U[l, i], DQ[j])
+            gq = nn(U[l, i], DQ[j, :, 0:256])
+            gv = nn(U[l, i], DQ[j, :, 512:768])
+            GB[l, j] += adapter_scale * jnp.where(top, gq, gv)
 
         x_copy(0, i).wait_send()
         SND[0, i] = (
-            nt(DQ[0], WQ[l, 0]) + nt(DQ[1], WQ[l, 1]) + nn(du, SP[l, 0, 8:16, :].astype(BF16))
+            nt(DQ[0], WQ[l, 0]) + nt(DQ[1], WQ[l, 1]) + tn(du, SP[l, 0, 8:16, :].astype(BF16))
         ).astype(BF16)
 
         @pl.when((l == 1) | (i != own_i))
         def _():
             x_copy(0, i).start()
+
+    def core_copies(l):
+        return (
+            pltpu.make_async_remote_copy(
+                GA.at[l], GCA, gc_s.at[0], gc_r.at[0], device_id=sib, device_id_type=MESH),
+            pltpu.make_async_remote_copy(
+                GB.at[l], GCB, gc_s.at[1], gc_r.at[1], device_id=sib, device_id_type=MESH),
+        )
+
+    def plane_copies(l):
+        out = []
+        for k, (dx, dy) in enumerate(((1, 0), (0, 1), (1, 1))):
+            x2 = 1 - x if dx else x
+            y2 = 1 - y if dy else y
+            to = (s, d, y2 * 2 + x2)
+            out.append(pltpu.make_async_remote_copy(
+                GA.at[l], GXA.at[k], gx_s.at[k], gx_r.at[k], device_id=to, device_id_type=MESH))
+        out.append(pltpu.make_async_remote_copy(
+            GB.at[l, 1 - y], GXB, gx_s.at[3], gx_r.at[3], device_id=yp, device_id_type=MESH))
+        return out
+
+    def line_copies():
+        out = []
+        for k in range(1, dp_count):
+            to = (s, lax.rem(d + k, dp_count), t)
+            out.append(pltpu.make_async_remote_copy(
+                GZA.at[d], GZA.at[d], gz_s.at[0, k - 1], gz_r.at[0, k - 1], device_id=to, device_id_type=MESH))
+            out.append(pltpu.make_async_remote_copy(
+                GZB.at[d], GZB.at[d], gz_s.at[1, k - 1], gz_r.at[1, k - 1], device_id=to, device_id_type=MESH))
+        return out
+
+    def sum_core(l):
+        @pl.when(s != l)
+        def _():
+            for c in core_copies(l):
+                c.start()
+
+    def sum_plane(l):
+        @pl.when(s == l)
+        def _():
+            for c in core_copies(l):
+                c.wait_recv()
+            GA[l] += GCA[...]
+            GB[l] += GCB[...]
+            for c in plane_copies(l):
+                c.start()
+
+    def sum_line(l):
+        @pl.when(s == l)
+        def _():
+            for c in plane_copies(l):
+                c.wait_recv()
+            GZA[d] = (GA[l] + GXA[0]) + (GXA[1] + GXA[2])
+            GZB[d] = GB[l, y] + GXB[...]
+            for c in line_copies():
+                c.start()
+
+    def sum_end(l):
+        @pl.when(s == l)
+        def _():
+            for c in line_copies():
+                c.wait_recv()
+            total_a, total_b = GZA[0], GZB[0]
+            for k in range(1, dp_count):
+                total_a, total_b = total_a + GZA[k], total_b + GZB[k]
+            out_a[0, 0] = total_a[0:4]
+            out_a[0, 1] = total_a[4:8]
+            out_b[0, 0] = total_b[0:4]
+            out_b[0, 1] = total_b[4:8]
 
     def bwd_layer(back, carry):
         l = 1 - back
 
         def f_turn(k, c):
+            @pl.when((l == 0) & (k == 1))
+            def _():
+                sum_plane(1)
+
             backward_ff(l, 1 - k)
             return c
 
         def a_turn(k, c):
+            @pl.when((l == 0) & (k == 0))
+            def _():
+                sum_line(1)
+
+            @pl.when((l == 0) & (k == 1))
+            def _():
+                sum_end(1)
+
             backward_attention(l, 1 - k)
             return c
 
@@ -971,9 +1201,11 @@
             finish_forward()
 
         lax.fori_loop(0, 2, a_turn, 0)
+        sum_core(l)
         return carry
 
     lax.fori_loop(0, 2, bwd_layer, 0)
+    sum_plane(0)
 
     x_copy(0, own_i).wait_recv()
 
@@ -983,17 +1215,27 @@
 
     by_rows(rows_out)
     send_result(3, 0, AB)
+    sum_line(0)
 
     x_copy(0, 1 - own_i).wait_send()
     for i in range(2):
         x_copy(1, i).wait_send()
     x_copy(2, 1 - own_i).wait_send()
+    def sent(ref, sem):
+        pltpu.make_async_remote_copy(ref, ref, sem, sem, device_id=sib, device_id_type=MESH).wait_send()
+
     for p in range(5):
-        w_sib(p).wait_send()
-        w_y(p).wait_send()
-        w_forward(p).wait_send()
-    spread_done(tok, H.at[0], 0)
-    spread_done(cot, DY, 1)
+        sent(pieces[p][1].at[s, y] if p else SP.at[s, y], ws_s.at[p])
+        for c in range(pieces[p][2] if p else 1):
+            k = base[p] + c
+            ref = block(p, s, y, chunk(p, c, 0)) if p else SP.at[s, y]
+            sent(ref, wy_s.at[k])
+            sent(ref, wa_s.at[k])
+            if p:
+                sent(ref, wz_s.at[k])
+                sent(ref, wb_s.at[k])
+    rows_done(tok, H.at[0], 0)
+    rows_done(cot, DY, 1)
     for l in range(2):
         kv_copy(l, 0).wait_send()
 
@@ -1009,6 +1251,16 @@
     @pl.when(s == 1)
     def _():
         dr_copy(0, 0).wait_send()
+
+    @pl.when(s == 0)
+    def _():
+        for c in core_copies(1) + tuple(plane_copies(0)) + tuple(line_copies()):
+            c.wait_send()
+
+    @pl.when(s == 1)
+    def _():
+        for c in core_copies(0) + tuple(plane_copies(1)) + tuple(line_copies()):
+            c.wait_send()
 
     send_result_done(0, 0, H.at[1, 0])
     send_result_done(1, 1, H.at[1, 0])
@@ -1017,6 +1269,7 @@
     for o, ref in ((0, act), (1, ig)):
         for m in range(2):
             pltpu.make_async_copy(tok.at[0], ref.at[m], out_rcv.at[o, m]).wait()
+    sum_end(0)
 
 
 def per_pair(
@@ -1024,47 +1277,22 @@
     query_value_bias, output_weight, upward_weight, upward_bias, down_weight, output_bias,
     adapter_down, adapter_upper,
 ):
-    gains, shifts, biases = norm_gain_pairs[0], norm_bias_pairs[0], output_bias[0]
-    vectors = jnp.stack([gains[0], shifts[0], gains[1], shifts[1], biases[0], biases[1]])
-    bias_qv = query_value_bias[0]
-    width = bias_qv.shape[1]
-    upper = adapter_upper[0]
-    rank = upper.shape[1]
-    empty = jnp.zeros((1, width), BF16)
-    qkv_bias = jnp.concatenate([bias_qv[0:1], empty, bias_qv[1:2], empty], axis=1)
-    none = jnp.zeros((rank, width), BF16)
-    upper_rows = jnp.concatenate(
-        [
-            jnp.concatenate([upper[0], none, none, none], axis=1),
-            jnp.concatenate([none, none, upper[1], none], axis=1),
-        ]
-    )
-    down_rows = adapter_down[0].reshape(2 * rank, D)
-    small = jnp.concatenate(
-        [
-            vectors,
-            jnp.zeros((2, D), BF16),
-            down_rows,
-            upward_bias[0][None],
-            qkv_bias,
-            jnp.zeros((6, D), BF16),
-            upper_rows,
-        ]
-    ).astype(F32)
-    weight_qkv = query_key_value_weight[0].reshape(D, 3 * width)
+    weight_qkv = query_key_value_weight[0].transpose(1, 0, 2)
+    dp_count = lax.axis_size("dp")
     anywhere = pl.BlockSpec(memory_space=pl.ANY)
     scalars = pl.BlockSpec(memory_space=pltpu.SMEM)
     vmem = pl.BlockSpec(memory_space=pltpu.VMEM)
     dma = pltpu.SemaphoreType.DMA
-    act, ig, ga, gb = pl.pallas_call(
-        fused_kernel,
+    act, ig, total_a, total_b = pl.pallas_call(
+        partial(fused_kernel, dp_count),
         out_shape=(
             jax.ShapeDtypeStruct((2, R, D), BF16),
             jax.ShapeDtypeStruct((2, R, D), BF16),
-            jax.ShapeDtypeStruct((2, 8, D), F32),
-            jax.ShapeDtypeStruct((2, 2, 8, 768), F32),
+            jax.ShapeDtypeStruct((1, 2, 4, D), F32),
+            jax.ShapeDtypeStruct((1, 2, 4, 256), F32),
         ),
-        in_specs=[anywhere, anywhere, scalars, scalars] + [anywhere] * 5,
+        in_specs=[anywhere, anywhere, scalars, scalars, vmem, vmem, anywhere, vmem, anywhere, anywhere, vmem,
+                  anywhere, vmem, vmem, vmem],
         out_specs=(anywhere, anywhere, vmem, vmem),
         scratch_shapes=[
             pltpu.VMEM((2, 2, 32, D), F32),
@@ -1081,25 +1309,37 @@
             pltpu.VMEM((2, 2, 512, R), BF16),
             pltpu.VMEM((2, 2, 8, 1, R), F32),
             pltpu.VMEM((3, 2, R, D), BF16),
-            pltpu.VMEM((3, 2, R, D), BF16),
-            pltpu.VMEM((R, D), F32),
-            pltpu.VMEM((2, 4 * R, R), F32),
-            pltpu.VMEM((2, 4 * R, R), BF16),
-            pltpu.VMEM((2, 4 * R, 512), F32),
-            pltpu.VMEM((2, 2, R, 512), F32),
+            pltpu.VMEM((5, R, D), BF16),
+            pltpu.VMEM((4, 4 * R, R), F32),
+            pltpu.VMEM((6 * R, R), BF16),
+            pltpu.VMEM((2, 4, R, R), F32),
             pltpu.VMEM((2, R, 768), BF16),
-            pltpu.VMEM((512, R), BF16),
-            pltpu.VMEM((R, 512), BF16),
             pltpu.VMEM((R, D), BF16),
-            pltpu.VMEM((2, 2, R, 8), BF16),
-            pltpu.VMEM((2, 128, R), F32),
+            pltpu.VMEM((2, 2, 8, R), BF16),
+            pltpu.VMEM((8, 64, R), F32),
+            pltpu.VMEM((16, R, R), BF16),
+            pltpu.VMEM((2, 8, D), F32),
+            pltpu.VMEM((2, 2, 8, 256), F32),
+            pltpu.VMEM((8, D), F32),
+            pltpu.VMEM((2, 8, 256), F32),
+            pltpu.VMEM((3, 8, D), F32),
+            pltpu.VMEM((8, 256), F32),
+            pltpu.VMEM((dp_count, 8, D), F32),
+            pltpu.VMEM((dp_count, 8, 256), F32),
             dma((2, 2)),
-            dma((2, 3)),
-            dma((2, 2, 5)),
+            dma((2,)),
+            dma((2,)),
             dma((5,)),
             dma((5,)),
             dma((5,)),
-            dma((5,)),
+            dma((8,)),
+            dma((8,)),
+            dma((7,)),
+            dma((7,)),
+            dma((8,)),
+            dma((8,)),
+            dma((7,)),
+            dma((7,)),
             dma((2, 2)),
             dma((2, 2)),
             dma((3, 2)),
@@ -1108,26 +1348,22 @@
             dma((2,)),
             dma((2, 2)),
             dma((4,)),
+            dma((2,)),
+            dma((2,)),
+            dma((4,)),
+            dma((4,)),
+            dma((2, dp_count - 1)),
+            dma((2, dp_count - 1)),
         ],
         compiler_params=pltpu.CompilerParams(
-            collective_id=0, has_side_effects=True, vmem_limit_bytes=63 * 2**20
+            collective_id=0, has_side_effects=True, vmem_limit_bytes=127 * 2**19
         ),
         name="two_layers",
     )(
-        tokens, cotangent, buckets, lengths, small, weight_qkv, output_weight[0],
-        upward_weight[0], down_weight[0],
+        tokens, cotangent, buckets, lengths, norm_gain_pairs, norm_bias_pairs, weight_qkv, query_value_bias,
+        output_weight, upward_weight, upward_bias, down_weight, output_bias, adapter_down, adapter_upper,
     )
-    s = lax.axis_index("section")
-    t = lax.axis_index("tensor")
-    part = jnp.stack([gb[:, :, 0:rank, 0:width], gb[:, :, rank : 2 * rank, 2 * width : 3 * width]], axis=1)
-    x = t % 2
-    zero = jnp.zeros_like(part)
-    both = jnp.where(x == 0, jnp.stack([part, zero], axis=3), jnp.stack([zero, part], axis=3))
-    wide = both.transpose(0, 1, 4, 2, 3, 5).reshape(2, 2, rank, 4 * width)
-    sums = lax.psum(jnp.stack([ga.reshape(2, 2, rank, D), wide]), ("section", "dp", "tensor"))
-    mine = lax.dynamic_index_in_dim(sums, s, 1, keepdims=False)
-    total_b = lax.dynamic_slice_in_dim(mine[1], t * width, width, 2)
-    return act[None], ig[None], mine[0][None], total_b[None]
+    return act[None], ig[None], total_a, total_b
 
 
 def solution(mesh):
@@ -1154,7 +1390,7 @@
         P("section", None, None, None),
         P("section", None, None, "tensor"),
     )
-    pairs = mesh.shape["section"] == 2 and mesh.shape["tensor"] == 4
+    pairs = mesh.shape["section"] == 2 and mesh.shape["tensor"] == 4 and mesh.shape["dp"] % 2 == 0
     return jax.shard_map(
         per_pair if pairs else per_device, mesh=mesh, in_specs=in_specs, out_specs=out_specs, check_vma=False
     )

time: 476 us -> 260 us (0.55)
  waiting for transfers between devices: 127 us -> 0 us
  Pallas kernels: 319 us -> 252 us
  between operations: 14.2 us -> 0.67 us
  local copies, waits for them, and re-layouts: 14.5 us -> 4.54 us
    psum x1 -> x0, waiting for transfers between devices: 127 us -> none  [per_pair(): lax.psum(jnp.stack([ga.reshape(2, 2, rank, D), wide]), ('section', 'dp',...]
    pallas_call x1, Pallas kernels: 319 us -> 252 us  [per_pair(): pl.pallas_call(partial(fused_kernel, dp_count), out_shape=(jax.ShapeDtype...]
  transfers between devices with their start and end apart: 1 -> 0, of which waited for: 1 -> 0; matrix products, arithmetic and copies ran while one was open for 0% -> 0% of each run, Pallas kernels for 0% -> 0%
where the time goes in v2:
time: 260 us; the launch traced here: 257 us
  Pallas kernels  252 us (97%)
  local copies, waits for them, and re-layouts  4.54 us (2%)
    pallas_call x1, Pallas kernels, per_pair(): pl.pallas_call(partial(fused_kernel, dp_count), out_shape=(jax.ShapeDtype...  252 us

profile of v2, /device:TPU:0, one launch (start us, length us, event | category | flops | bytes accessed | tf_op | source)
XLA Modules:
  0.0 257.4 jit_solution(10132402070612282551)
XLA Ops:
  0.6 252.2 %two_layers.1 = (bf16[2,256,1024]{2,1,0:T(8,128)(2,1)}, bf16[2,256,1024]{2,1,0:T(8,128)(2,1)}, f32[1,2,4,1024]{3,2,1,0:T(4,128)}, f32[1,2,4,256]{3,2,1,0:T(4,128)}) custom-call(bf16[2,256,1024]{2,1,0:T(8,128)(2,1)} %tok.1, bf16[2,256,1024]{2,1,0:T(8,128)(2,1)} %cot.1, s32[2]{0:T(128)} %buckets.1, s32[2,8]{1,0:T(2,128)} %lengths.1, ...), custom_call_target="tpu_custom_call" | custom-call | tf_op jit(solution)/shard_map/two_layers/pallas_call | solution.py:1286
  252.8 0.0 copy-start
  252.9 0.0 copy-start.1
  252.9 0.0 copy-start.2
  252.9 2.3 copy.23
  255.2 0.0 copy-done
  255.2 1.0 copy.24
  256.2 0.0 copy-done.1
  256.2 0.6 copy.25
  256.8 0.0 copy-done.2
  256.8 0.6 copy.26
Async XLA Ops:
  252.8 2.4 copy-start
  252.9 3.3 %copy-start.1 = (f32[1,2,4,1024]{3,2,1,0:T(4,128)S(1)}, f32[1,2,4,1024]{3,2,1,0:T(4,128)}, u32[]{:S(2)}) copy-start(f32[1,2,4,1024]{3,2,1,0:T(4,128)} %get-tuple-element.18) | copy-start | bytes 98308
  252.9 4.0 %copy-start.2 = (f32[1,2,4,256]{3,2,1,0:T(4,128)S(1)}, f32[1,2,4,256]{3,2,1,0:T(4,128)}, u32[]{:S(2)}) copy-start(f32[1,2,4,256]{3,2,1,0:T(4,128)} %get-tuple-element.19) | copy-start | bytes 24580

commit v3 on v2

--- a/solution.py
+++ b/solution.py
@@ -398,7 +398,7 @@
     SP, WQ, WO, WU, WD, H, DY, MID, GP, Q, KV, OT, LSE, SND, RCV, BIG, MSK, DR, DQ, AB, U, OACC, PB,
     GA, GB, GCA, GCB, GXA, GXB, GZA, GZB,
     tok_sem, tok_ys, tok_xs, wl, ws_r, ws_s, wy_r, wy_s, wz_r, wz_s, wa_r, wa_s, wb_r, wb_s,
-    kv_rcv, kv_snd, x_rcv, x_snd, dr_rcv, dr_snd, out_rcv, out_snd, gc_r, gc_s, gx_r, gx_s, gz_r, gz_s,
+    kv_rcv, kv_snd, x_rcv, x_snd, last_rcv, last_snd, dr_rcv, dr_snd, out_rcv, out_snd, gc_r, gc_s, gx_r, gx_s, gz_r, gz_s,
 ):
     s = lax.axis_index("section")
     d = lax.axis_index("dp")
@@ -448,14 +448,18 @@
 
         return local, to_y, first_x, then_x
 
-    def rows_start(src, dst, w):
-        local, to_y, first_x, _ = row_copies(src, dst, w)
+    def rows_first(src, dst, w):
+        local, _, first_x, _ = row_copies(src, dst, w)
 
         @pl.when(y == own_i)
         def _():
             first_x().start()
-            to_y().start()
             local().start()
+
+    def rows_swap(src, dst, w):
+        @pl.when(y == own_i)
+        def _():
+            row_copies(src, dst, w)[1]().start()
 
     def rows_relay(src, dst, w):
         pltpu.make_async_copy(src.at[0], dst.at[own_i], tok_sem.at[w, own_i]).wait()
@@ -567,7 +571,8 @@
     def _():
         y_start(1)
 
-    rows_start(tok, H.at[0], 0)
+    rows_swap(tok, H.at[0], 0)
+    rows_first(tok, H.at[0], 0)
     SP[s, y] = jnp.zeros(SP.shape[2:], F32)
     for k, (ref, row) in enumerate(
         ((gain_in, 0), (shift_in, 0), (gain_in, 1), (shift_in, 1), (bo_in, 0), (bo_in, 1))
@@ -590,8 +595,6 @@
         for p in range(2, 5):
             y_start(p)
 
-    rows_start(cot, DY, 1)
-
     shift = 7 + buckets[y]
     span_mask = lax.shift_left(jnp.int32(1), shift) - 1
 
@@ -629,6 +632,12 @@
             SND.at[slot, i], RCV.at[slot * 2 + (i if slot < 2 else 0)], x_snd.at[slot, i], x_rcv.at[slot, i],
             device_id=xp, device_id_type=MESH)
 
+    def last_copy(c, i):
+        rows = slice(c * 64, c * 64 + 64)
+        return pltpu.make_async_remote_copy(
+            SND.at[0, i, rows, :], RCV.at[i, rows, :], last_snd.at[c], last_rcv.at[c],
+            device_id=xp, device_id_type=MESH)
+
     def by_rows(body):
         body(slice(0, R))
 
@@ -645,19 +654,20 @@
     def swapped(slot, i, rows):
         return SND[slot, i, rows, :].astype(F32) + RCV[slot * 2 + (i if slot < 2 else 0), rows, :].astype(F32)
 
-    def send_result(which, layer, src):
+    def send_result(which, layer, src, rows=slice(0, R)):
+        src = src.at[rows, :]
         dst = act if which < 2 else ig
         o = 0 if which < 2 else 1
         here = (s == layer) & (y == own_i)
 
         @pl.when(here)
         def _():
-            pltpu.make_async_copy(src, dst.at[y], out_rcv.at[o, y]).start()
+            pltpu.make_async_copy(src, dst.at[y, rows, :], out_rcv.at[o, y]).start()
 
         @pl.when(jnp.logical_not(here))
         def _():
             pltpu.make_async_remote_copy(
-                src, dst.at[y], out_snd.at[which], out_rcv.at[o, y],
+                src, dst.at[y, rows, :], out_snd.at[which], out_rcv.at[o, y],
                 device_id=(layer, d, own_i * 2 + x), device_id_type=MESH).start()
 
     def send_result_done(which, layer, src):
@@ -756,7 +766,12 @@
                 relay_y(l, 0)
                 relay_y(l, 1, 1)
                 relay_z(l, 1, 0)
-                rows_rest(tok, H.at[0], 0)
+
+                @pl.when(own_i == 1)
+                def _():
+                    rows_rest(tok, H.at[0], 0)
+
+                rows_first(cot, DY, 1)
 
             own_wait(l, 0)
             other_wait(l, 0)
@@ -764,6 +779,7 @@
 
             @pl.when(l == 1)
             def _():
+                rows_relay(cot, DY, 1)
                 relay_z(l, 1, 0)
 
             relay_y(l, 2)
@@ -772,6 +788,10 @@
 
         @pl.when(i == 1)
         def _():
+            @pl.when((l == 0) & (own_i == 0))
+            def _():
+                rows_rest(tok, H.at[0], 0)
+
             relay_y(l, 3, 0)
             relay_y(l, 3, 1)
 
@@ -850,8 +870,7 @@
 
         @pl.when((i == 1) & (l == 0))
         def _():
-            rows_relay(cot, DY, 1)
-            rows_rest(cot, DY, 1)
+            rows_swap(cot, DY, 1)
             relay_y(1, 0)
             relay_y(1, 1, 0)
             relay_y(1, 1, 1)
@@ -923,6 +942,10 @@
             @pl.when(i == own_i)
             def _():
                 row_copies(cot, DY, 1)[3]().wait_send()
+
+            @pl.when(i != own_i)
+            def _():
+                rows_rest(cot, DY, 1)
 
             def rows_valid(rows):
                 pos = blk_of(i) * R + lax.broadcasted_iota(jnp.int32, (R, 1), 0)
@@ -1098,9 +1121,14 @@
             nt(DQ[0], WQ[l, 0]) + nt(DQ[1], WQ[l, 1]) + tn(du, SP[l, 0, 8:16, :].astype(BF16))
         ).astype(BF16)
 
-        @pl.when((l == 1) | (i != own_i))
+        @pl.when(l == 1)
         def _():
             x_copy(0, i).start()
+
+        @pl.when((l == 0) & (i != own_i))
+        def _():
+            for c in range(4):
+                last_copy(c, i).start()
 
     def core_copies(l):
         return (
@@ -1207,17 +1235,16 @@
     lax.fori_loop(0, 2, bwd_layer, 0)
     sum_plane(0)
 
-    x_copy(0, own_i).wait_recv()
-
-    def rows_out(rows):
+    for c in range(4):
+        last_copy(c, own_i).wait_recv()
+        rows = slice(c * 64, c * 64 + 64)
         g = swapped(0, own_i, rows) * vec(0, 0)
         AB[rows, :] = (MID[0, own_i, rows, :] + norm_pull(H[0, own_i, rows, :].astype(F32), g)).astype(BF16)
-
-    by_rows(rows_out)
-    send_result(3, 0, AB)
+        send_result(3, 0, AB, rows)
     sum_line(0)
 
-    x_copy(0, 1 - own_i).wait_send()
+    for c in range(4):
+        last_copy(c, 1 - own_i).wait_send()
     for i in range(2):
         x_copy(1, i).wait_send()
     x_copy(2, 1 - own_i).wait_send()
@@ -1344,6 +1371,8 @@
             dma((2, 2)),
             dma((3, 2)),
             dma((3, 2)),
+            dma((4,)),
+            dma((4,)),
             dma((2,)),
             dma((2,)),
             dma((2, 2)),

time: 260 us -> 244 us (0.938)
  Pallas kernels: 252 us -> 239 us
    pallas_call x1, Pallas kernels: 252 us -> 239 us  [per_pair(): pl.pallas_call(partial(fused_kernel, dp_count), out_shape=(jax.ShapeDtype...]
where the time goes in v3:
time: 244 us
  Pallas kernels  239 us (98%)
  local copies, waits for them, and re-layouts  4.54 us (2%)
    pallas_call x1, Pallas kernels, per_pair(): pl.pallas_call(partial(fused_kernel, dp_count), out_shape=(jax.ShapeDtype...  239 us

profile of v3, /device:TPU:0, one launch (start us, length us, event | category | flops | bytes accessed | tf_op | source)
XLA Modules:
  0.0 243.9 jit_solution(3628560194348653764)
XLA Ops:
  0.6 238.7 %two_layers.1 = (bf16[2,256,1024]{2,1,0:T(8,128)(2,1)}, bf16[2,256,1024]{2,1,0:T(8,128)(2,1)}, f32[1,2,4,1024]{3,2,1,0:T(4,128)}, f32[1,2,4,256]{3,2,1,0:T(4,128)}) custom-call(bf16[2,256,1024]{2,1,0:T(8,128)(2,1)} %tok.1, bf16[2,256,1024]{2,1,0:T(8,128)(2,1)} %cot.1, s32[2]{0:T(128)} %buckets.1, s32[2,8]{1,0:T(2,128)} %lengths.1, ...), custom_call_target="tpu_custom_call" | custom-call | tf_op jit(solution)/shard_map/two_layers/pallas_call | solution.py:1313
  239.4 0.0 copy-start
  239.4 0.0 copy-start.1
  239.4 0.0 copy-start.2
  239.4 2.3 copy.23
  241.7 0.0 copy-done
  241.7 1.0 copy.24
  242.7 0.0 copy-done.1
  242.7 0.6 copy.25
  243.3 0.0 copy-done.2
  243.3 0.6 copy.26
Async XLA Ops:
  239.4 2.4 copy-start
  239.4 3.3 %copy-start.1 = (f32[1,2,4,1024]{3,2,1,0:T(4,128)S(1)}, f32[1,2,4,1024]{3,2,1,0:T(4,128)}, u32[]{:S(2)}) copy-start(f32[1,2,4,1024]{3,2,1,0:T(4,128)} %get-tuple-element.18) | copy-start | bytes 98308
  239.4 4.0 %copy-start.2 = (f32[1,2,4,256]{3,2,1,0:T(4,128)S(1)}, f32[1,2,4,256]{3,2,1,0:T(4,128)}, u32[]{:S(2)}) copy-start(f32[1,2,4,256]{3,2,1,0:T(4,128)} %get-tuple-element.19) | copy-start | bytes 24580

commit v4 on v3

--- a/solution.py
+++ b/solution.py
@@ -480,8 +480,11 @@
         def _():
             to_y().wait_send()
 
-    pieces = (None, (wq_in, WQ, 2), (wo_in, WO, 1), (wu_in, WU, 2), (wd_in, WD, 2))
-    base = (7, 0, 2, 3, 5)
+    pieces = (None, (wq_in, WQ, 4), (wo_in, WO, 1), (wu_in, WU, 4), (wd_in, WD, 4))
+    base = (13, 0, 4, 5, 9)
+
+    def relayer(l, c):
+        return 1 - l if c % 2 else l
 
     def sources(p, rows):
         src, dst, _ = pieces[p]
@@ -506,41 +509,66 @@
             pltpu.make_async_remote_copy(
                 src, dst, ws_s.at[p], ws_r.at[p], device_id=sib, device_id_type=MESH).start()
 
-    def y_start(p):
-        if p == 0:
-            small_copy(yp, wy_s.at[7], wy_r.at[7]).start()
-            return
-        for c in range(pieces[p][2]):
-            for src, dst in sources(p, chunk(p, c, z_half)):
-                k = base[p] + c
-                pltpu.make_async_remote_copy(
-                    src, dst, wy_s.at[k], wy_r.at[k], device_id=yp, device_id_type=MESH).start()
+    def whole_by_y(l, p, c):
+        return l == 0 and p == 4 and c >= 2
+
+    def y_start(l, p):
+        for c in range(pieces[p][2] if p else 1):
+            k = base[p] + c
+
+            @pl.when(s == relayer(l, c))
+            def _():
+                if p == 0:
+                    ref = SP.at[l, y, 16:32, :]
+                    pltpu.make_async_remote_copy(
+                        ref, ref, wy_s.at[k], wy_r.at[k], device_id=yp, device_id_type=MESH).start()
+                    return
+                rows = chunk(p, c, z_half)
+                mine = block(p, l, y, rows)
+                for src, dst in [(mine, mine)] if c % 2 else sources(p, rows):
+                    pltpu.make_async_remote_copy(
+                        src, dst, wy_s.at[k], wy_r.at[k], device_id=yp, device_id_type=MESH).start()
+                if whole_by_y(l, p, c):
+                    rows = chunk(p, c, 1 - z_half)
+                    mine = block(p, l, y, rows)
+                    for src, dst in [(mine, mine)] if c % 2 else sources(p, rows):
+                        pltpu.make_async_remote_copy(
+                            src, dst, wz_s.at[k], wz_r.at[k], device_id=yp, device_id_type=MESH).start()
 
     def small_copy(to, snd, rcv):
         return pltpu.make_async_remote_copy(
             SP.at[s, y], SP.at[s, y], snd, rcv, device_id=to, device_id_type=MESH)
 
-    def passed(p, c, half, to, snd, rcv):
-        ref = SP.at[s, 1 - y] if p == 0 else block(p, s, 1 - y, chunk(p, c, half))
+    def passed(l, p, c, half, to, snd, rcv):
+        ref = SP.at[l, 1 - y, 16:32, :] if p == 0 else block(p, l, 1 - y, chunk(p, c, half))
         return pltpu.make_async_remote_copy(ref, ref, snd, rcv, device_id=to, device_id_type=MESH)
 
-    def relay_y(l, p, c=0):
-        k = base[p] + c
-
-        @pl.when(l == s)
-        def _():
-            passed(p, c, z_half, sib, wa_s.at[k], wy_r.at[k]).wait_recv()
-            if p:
-                passed(p, c, z_half, zp, wz_s.at[k], wz_r.at[k]).start()
-            passed(p, c, z_half, sib, wa_s.at[k], wa_r.at[k]).start()
-
-    def relay_z(l, p, c=0):
-        k = base[p] + c
-
-        @pl.when(l == s)
-        def _():
-            passed(p, c, 1 - z_half, zp, wz_s.at[k], wz_r.at[k]).wait_recv()
-            passed(p, c, 1 - z_half, sib, wb_s.at[k], wb_r.at[k]).start()
+    def relay_y(l, p):
+        for c in range(pieces[p][2] if p else 1):
+            k = base[p] + c
+
+            @pl.when(s == relayer(l, c))
+            def _():
+                passed(l, p, c, z_half, sib, wa_s.at[k], wy_r.at[k]).wait_recv()
+                if p and not (p == 4 and c >= 2):
+                    passed(l, p, c, z_half, zp, wz_s.at[k], wz_r.at[k]).start()
+
+                if p == 4 and c >= 2:
+
+                    @pl.when(l == 1)
+                    def _():
+                        passed(l, p, c, z_half, zp, wz_s.at[k], wz_r.at[k]).start()
+
+                passed(l, p, c, z_half, sib, wa_s.at[k], wa_r.at[k]).start()
+
+    def relay_z(l, p):
+        for c in range(pieces[p][2]):
+            k = base[p] + c
+
+            @pl.when(s == relayer(l, c))
+            def _():
+                passed(l, p, c, 1 - z_half, zp, wz_s.at[k], wz_r.at[k]).wait_recv()
+                passed(l, p, c, 1 - z_half, sib, wb_s.at[k], wb_r.at[k]).start()
 
     def own_wait(l, p):
         @pl.when(l == s)
@@ -555,24 +583,22 @@
             pltpu.make_async_copy(ref, ref, ws_r.at[p]).wait()
 
     def other_wait(l, p):
-        @pl.when(l != s)
-        def _():
-            if p == 0:
-                ref = SP.at[1 - s, 1 - y]
-                pltpu.make_async_copy(ref, ref, wa_r.at[7]).wait()
-            else:
-                for c in range(pieces[p][2]):
-                    k = base[p] + c
-                    ref = block(p, 1 - s, 1 - y, chunk(p, c, 0))
+        for c in range(pieces[p][2] if p else 1):
+            k = base[p] + c
+
+            @pl.when(s != relayer(l, c))
+            def _():
+                if p == 0:
+                    ref = SP.at[l, 1 - y, 16:32, :]
+                    pltpu.make_async_copy(ref, ref, wa_r.at[13]).wait()
+                else:
+                    ref = block(p, l, 1 - y, chunk(p, c, 0))
                     pltpu.make_async_copy(ref, ref, wa_r.at[k]).wait()
                     pltpu.make_async_copy(ref, ref, wb_r.at[k]).wait()
 
-    @pl.when(s == 0)
-    def _():
-        y_start(1)
-
     rows_swap(tok, H.at[0], 0)
     rows_first(tok, H.at[0], 0)
+    own_start(1)
     SP[s, y] = jnp.zeros(SP.shape[2:], F32)
     for k, (ref, row) in enumerate(
         ((gain_in, 0), (shift_in, 0), (gain_in, 1), (shift_in, 1), (bo_in, 0), (bo_in, 1))
@@ -586,14 +612,14 @@
     SP[s, y, 24:28, 0:256] = au_in[0, 0].astype(F32)
     SP[s, y, 28:32, 512:768] = au_in[0, 1].astype(F32)
     small_copy(sib, ws_s.at[0], ws_r.at[0]).start()
-    for p in range(1, 5):
+    y_start(0, 0)
+    for p in range(2, 5):
         own_start(p)
-
-    @pl.when(s == 0)
-    def _():
-        y_start(0)
-        for p in range(2, 5):
-            y_start(p)
+    for l in range(2):
+        for p in range(5):
+            own_wait(l, p)
+            if l or p:
+                y_start(l, p)
 
     shift = 7 + buckets[y]
     span_mask = lax.shift_left(jnp.int32(1), shift) - 1
@@ -682,7 +708,7 @@
                 device_id=(layer, d, own_i * 2 + x), device_id_type=MESH).wait_send()
 
     def vec(l, k):
-        return SP[l, 0, k : k + 1, :]
+        return SP[l, y, k : k + 1, :]
 
     def head_lanes(pair):
         return pl.ds(pl.multiple_of(pair * 128, 128), 128)
@@ -761,29 +787,23 @@
         def _():
             @pl.when(l == 0)
             def _():
-                relay_y(l, 1, 0)
                 rows_relay(tok, H.at[0], 0)
                 relay_y(l, 0)
-                relay_y(l, 1, 1)
-                relay_z(l, 1, 0)
+                relay_y(l, 1)
+                rows_first(cot, DY, 1)
 
                 @pl.when(own_i == 1)
                 def _():
                     rows_rest(tok, H.at[0], 0)
 
-                rows_first(cot, DY, 1)
-
-            own_wait(l, 0)
             other_wait(l, 0)
-            own_wait(l, 1)
+            relay_z(l, 1)
 
             @pl.when(l == 1)
             def _():
-                rows_relay(cot, DY, 1)
-                relay_z(l, 1, 0)
-
-            relay_y(l, 2)
-            relay_z(l, 1, 1)
+                relay_y(l, 2)
+                relay_y(l, 3)
+
             other_wait(l, 1)
 
         @pl.when(i == 1)
@@ -792,8 +812,6 @@
             def _():
                 rows_rest(tok, H.at[0], 0)
 
-            relay_y(l, 3, 0)
-            relay_y(l, 3, 1)
 
         @pl.when(l == 1)
         def _():
@@ -814,8 +832,8 @@
             AB[rows, :] = (xhat * vec(l, 0) + vec(l, 1)).astype(BF16)
 
         by_rows(rows_norm)
-        u = nt(AB[...], SP[l, 0, 8:16, :].astype(BF16)).astype(BF16)
-        U[l, i] = nt(SP[l, 0, 8:16, :].astype(BF16), AB[...]).astype(BF16)
+        u = nt(AB[...], SP[l, y, 8:16, :].astype(BF16)).astype(BF16)
+        U[l, i] = nt(SP[l, y, 8:16, :].astype(BF16), AB[...]).astype(BF16)
         own_rows = pl.ds(pl.multiple_of(b * R, R), R)
         for j in range(2):
             up = SP[l, j, 24:32, 0:768].astype(BF16)
@@ -838,11 +856,24 @@
             kv_wait(l, 0)
             kv_wait(l, 1)
 
+        @pl.when((i == 0) & (l == 0))
+        def _():
+            relay_y(l, 2)
+
+        @pl.when(i == 1)
+        def _():
+            @pl.when(l == 0)
+            def _():
+                relay_y(l, 3)
+
+            @pl.when(l == 1)
+            def _():
+                relay_y(l, 4)
+
         attend(l, i)
 
         @pl.when(i == 0)
         def _():
-            own_wait(l, 2)
             relay_z(l, 2)
             other_wait(l, 2)
 
@@ -854,26 +885,17 @@
         x_copy(0, i).start()
 
     def forward_ff(l, i):
-        @pl.when(i == 0)
-        def _():
-            @pl.when((s == 1) & (l == 0))
-            def _():
-                for p in range(5):
-                    y_start(p)
-
-            own_wait(l, 3)
-            own_wait(l, 4)
-            relay_z(l, 3, 0)
-            relay_y(l, 4, 0)
-            relay_z(l, 3, 1)
-            relay_y(l, 4, 1)
+        @pl.when((i == 0) & (l == 0))
+        def _():
+            relay_y(l, 4)
 
         @pl.when((i == 1) & (l == 0))
         def _():
             rows_swap(cot, DY, 1)
-            relay_y(1, 0)
-            relay_y(1, 1, 0)
-            relay_y(1, 1, 1)
+
+        @pl.when((i == 1) & (l == 1))
+        def _():
+            rows_relay(cot, DY, 1)
 
         x_copy(0, i).wait_recv()
 
@@ -891,8 +913,8 @@
 
                 @pl.when(i == 0)
                 def _():
-                    relay_z(l, 4, 0)
-                    relay_z(l, 4, 1)
+                    relay_z(l, 3)
+                    relay_z(l, 4)
                     other_wait(l, 3)
                     other_wait(l, 4)
 
@@ -906,6 +928,11 @@
         @pl.when(l == 0)
         def _():
             x_copy(1, i).start()
+
+            @pl.when(i == 1)
+            def _():
+                relay_y(1, 0)
+                relay_y(1, 1)
 
         @pl.when((l == 1) & (i != own_i))
         def _():
@@ -1118,7 +1145,7 @@
 
         x_copy(0, i).wait_send()
         SND[0, i] = (
-            nt(DQ[0], WQ[l, 0]) + nt(DQ[1], WQ[l, 1]) + tn(du, SP[l, 0, 8:16, :].astype(BF16))
+            nt(DQ[0], WQ[l, 0]) + nt(DQ[1], WQ[l, 1]) + tn(du, SP[l, y, 8:16, :].astype(BF16))
         ).astype(BF16)
 
         @pl.when(l == 1)
@@ -1255,7 +1282,7 @@
         sent(pieces[p][1].at[s, y] if p else SP.at[s, y], ws_s.at[p])
         for c in range(pieces[p][2] if p else 1):
             k = base[p] + c
-            ref = block(p, s, y, chunk(p, c, 0)) if p else SP.at[s, y]
+            ref = block(p, s, y, chunk(p, c, 0)) if p else SP.at[s, y, 16:32, :]
             sent(ref, wy_s.at[k])
             sent(ref, wa_s.at[k])
             if p:
@@ -1297,6 +1324,38 @@
         for m in range(2):
             pltpu.make_async_copy(tok.at[0], ref.at[m], out_rcv.at[o, m]).wait()
     sum_end(0)
+
+
+def copy_kernel(a_in, g_in, ta_in, tb_in, a_out, g_out, ta_out, tb_out, held_a, held_g, held_ta, held_tb, load, store):
+    moves = []
+    for k, (src, held, dst) in enumerate(((a_in, held_a, a_out), (g_in, held_g, g_out))):
+        for m in range(src.shape[0]):
+            moves.append((src.at[m], held.at[m], dst.at[0, m], 2 * k + m))
+    moves.append((ta_in, held_ta, ta_out, 4))
+    moves.append((tb_in, held_tb, tb_out, 5))
+    for src, held, dst, k in moves:
+        pltpu.make_async_copy(src, held, load.at[k]).start()
+    for src, held, dst, k in moves:
+        pltpu.make_async_copy(src, held, load.at[k]).wait()
+        pltpu.make_async_copy(held, dst, store.at[k]).start()
+    for src, held, dst, k in moves:
+        pltpu.make_async_copy(held, dst, store.at[k]).wait()
+
+
+def settle(act, ig, total_a, total_b):
+    anywhere = pl.BlockSpec(memory_space=pl.ANY)
+    shapes = [(1,) + act.shape, (1,) + ig.shape, total_a.shape, total_b.shape]
+    kinds = [act.dtype, ig.dtype, total_a.dtype, total_b.dtype]
+    return pl.pallas_call(
+        copy_kernel,
+        out_shape=tuple(jax.ShapeDtypeStruct(a, b) for a, b in zip(shapes, kinds)),
+        in_specs=[anywhere] * 4,
+        out_specs=(anywhere,) * 4,
+        scratch_shapes=[
+            pltpu.VMEM(v.shape, v.dtype) for v in (act, ig, total_a, total_b)
+        ] + [pltpu.SemaphoreType.DMA((6,))] * 2,
+        name="settle",
+    )(act, ig, total_a, total_b)
 
 
 def per_pair(
@@ -1359,14 +1418,14 @@
             dma((5,)),
             dma((5,)),
             dma((5,)),
-            dma((8,)),
-            dma((8,)),
-            dma((7,)),
-            dma((7,)),
-            dma((8,)),
-            dma((8,)),
-            dma((7,)),
-            dma((7,)),
+            dma((14,)),
+            dma((14,)),
+            dma((13,)),
+            dma((13,)),
+            dma((14,)),
+            dma((14,)),
+            dma((13,)),
+            dma((13,)),
             dma((2, 2)),
             dma((2, 2)),
             dma((3, 2)),
@@ -1392,7 +1451,7 @@
         tokens, cotangent, buckets, lengths, norm_gain_pairs, norm_bias_pairs, weight_qkv, query_value_bias,
         output_weight, upward_weight, upward_bias, down_weight, output_bias, adapter_down, adapter_upper,
     )
-    return act[None], ig[None], total_a, total_b
+    return settle(act, ig, total_a, total_b)
 
 
 def solution(mesh):

time: 244 us -> 233 us (0.955)
  Pallas kernels: 239 us -> 232 us
  local copies, waits for them, and re-layouts: 4.54 us -> 0 us
    pallas_call x1, Pallas kernels: 239 us -> 229 us  [per_pair(): pl.pallas_call(partial(fused_kernel, dp_count), out_shape=(jax.ShapeDtype...]
    unnamed x10 -> x0, local copies, waits for them, and re-layouts: 4.54 us -> none
    pallas_call x0 -> x1, Pallas kernels: none -> 2.46 us  [settle(): pl.pallas_call(copy_kernel, out_shape=tuple((jax.ShapeDtypeStruct(a, b) f...]
where the time goes in v4:
time: 233 us
  Pallas kernels  232 us (100%)
    pallas_call x1, Pallas kernels, per_pair(): pl.pallas_call(partial(fused_kernel, dp_count), out_shape=(jax.ShapeDtype...  229 us

profile of v4, /device:TPU:0, one launch (start us, length us, event | category | flops | bytes accessed | tf_op | source)
XLA Modules:
  0.0 232.6 jit_solution(14999956715902436614)
XLA Ops:
  0.6 229.4 %two_layers.1 = (bf16[2,256,1024]{2,1,0:T(8,128)(2,1)}, bf16[2,256,1024]{2,1,0:T(8,128)(2,1)}, f32[1,2,4,1024]{3,2,1,0:T(4,128)}, f32[1,2,4,256]{3,2,1,0:T(4,128)}) custom-call(bf16[2,256,1024]{2,1,0:T(8,128)(2,1)} %tok.1, bf16[2,256,1024]{2,1,0:T(8,128)(2,1)} %cot.1, s32[2]{0:T(128)} %buckets.1, s32[2,8]{1,0:T(2,128)} %lengths.1, ...), custom_call_target="tpu_custom_call" | custom-call | tf_op jit(solution)/shard_map/two_layers/pallas_call | solution.py:1372
  230.0 2.5 %settle.1 = (bf16[1,2,256,1024]{3,2,1,0:T(8,128)(2,1)}, bf16[1,2,256,1024]{3,2,1,0:T(8,128)(2,1)}, f32[1,2,4,1024]{3,2,1,0:T(4,128)}, f32[1,2,4,256]{3,2,1,0:T(4,128)}) custom-call(bf16[2,256,1024]{2,1,0:T(8,128)(2,1)} %get-tuple-element.8.a_in, bf16[2,256,1024]{2,1,0:T(8,128)(2,1)} %get-tuple-element.9.g_in, f32[1,2,4,1024]{3,2,1,0:T(4,128)} %get-tuple-element.10.ta_in, ...), custom_call_target="tpu_custom_call" | custom-call | tf_op jit(solution)/shard_map/settle/pallas_call | solution.py:1349

commit v5 on v4

--- a/solution.py
+++ b/solution.py
@@ -833,19 +833,23 @@
 
         by_rows(rows_norm)
         u = nt(AB[...], SP[l, y, 8:16, :].astype(BF16)).astype(BF16)
-        U[l, i] = nt(SP[l, y, 8:16, :].astype(BF16), AB[...]).astype(BF16)
         own_rows = pl.ds(pl.multiple_of(b * R, R), R)
         for j in range(2):
-            up = SP[l, j, 24:32, 0:768].astype(BF16)
-            qkv = nn(AB[...], WQ[l, j]) + (adapter_scale * nn(u, up) + SP[l, j, 17:18, 0:768])
+            up = SP[l, j, 24:32, 256:768].astype(BF16)
             cols = slice(j * 256, j * 256 + 256)
-            Q[l, i, :, cols] = (qkv[:, 0:256] * HEAD_DIM ** -0.5).astype(BF16)
-            KV[l, 0, own_rows, cols] = qkv[:, 256:512].astype(BF16)
-            KV[l, 1, own_rows, cols] = qkv[:, 512:768].astype(BF16)
+            pair = nn(AB[...], WQ[l, j, :, 256:768]) + (adapter_scale * nn(u, up) + SP[l, j, 17:18, 256:768])
+            KV[l, 0, own_rows, cols] = pair[:, 0:256].astype(BF16)
+            KV[l, 1, own_rows, cols] = pair[:, 256:512].astype(BF16)
 
         @pl.when(b != 3)
         def _():
             kv_copy(l, i).start()
+
+        for j in range(2):
+            up = SP[l, j, 24:32, 0:256].astype(BF16)
+            q = nn(AB[...], WQ[l, j, :, 0:256]) + (adapter_scale * nn(u, up) + SP[l, j, 17:18, 0:256])
+            Q[l, i, :, j * 256 : j * 256 + 256] = (q * HEAD_DIM ** -0.5).astype(BF16)
+        U[l, i] = nt(SP[l, y, 8:16, :].astype(BF16), AB[...]).astype(BF16)
 
         @pl.when((s == 1) & (i == 0))
         def _():
@@ -1056,6 +1060,12 @@
                 keys = jnp.transpose(KV[l, 0, rows, k * 128 : k * 128 + 128])
                 for e in range(2):
                     OACC[2 * k + e] += nn(keys[e * 64 : e * 64 + 64], PB[2 * k + e])
+            for k in range(2):
+
+                @pl.when((s == 0) & (i == 1) & (j == k + 1))
+                def _():
+                    dr_copy(k, k + 1).start()
+
             return c
 
         lax.fori_loop(0, b + 1, turn, 0)
@@ -1101,10 +1111,11 @@
         attend_back(l, i)
         own = pl.ds(pl.multiple_of(b * R, R), R)
 
-        @pl.when((s == 0) & (i == 1))
-        def _():
-            dr_copy(0, 1).start()
-            dr_copy(1, 2).start()
+        def rows_norm(rows):
+            xhat, _ = normalize(H[l, i, rows, :].astype(F32))
+            AB[rows, :] = (xhat * vec(l, 0) + vec(l, 1)).astype(BF16)
+
+        by_rows(rows_norm)
 
         @pl.when(b != 3)
         def _():
@@ -1129,11 +1140,6 @@
             DQ[j, :, 256:512] = BIG[j, own, :].astype(BF16)
             DQ[j, :, 512:768] = BIG[2 + j, own, :].astype(BF16)
 
-        def rows_norm(rows):
-            xhat, _ = normalize(H[l, i, rows, :].astype(F32))
-            AB[rows, :] = (xhat * vec(l, 0) + vec(l, 1)).astype(BF16)
-
-        by_rows(rows_norm)
         ups = [SP[l, j, 24:32, 0:768].astype(BF16) for j in range(2)]
         du = (adapter_scale * (nt(ups[0], DQ[0]) + nt(ups[1], DQ[1]))).astype(BF16)
         GA[l] += nn(du, AB[...])

time: 233 us -> 230 us (0.987)
  Pallas kernels: 232 us -> 229 us
    pallas_call x1, Pallas kernels: 229 us -> 226 us  [per_pair(): pl.pallas_call(partial(fused_kernel, dp_count), out_shape=(jax.ShapeDtype...]
where the time goes in v5:
time: 230 us
  Pallas kernels  229 us (100%)
    pallas_call x1, Pallas kernels, per_pair(): pl.pallas_call(partial(fused_kernel, dp_count), out_shape=(jax.ShapeDtype...  226 us

profile of v5, /device:TPU:0, one launch (start us, length us, event | category | flops | bytes accessed | tf_op | source)
XLA Modules:
  0.0 229.5 jit_solution(7676048573906296312)
XLA Ops:
  0.6 226.2 %two_layers.1 = (bf16[2,256,1024]{2,1,0:T(8,128)(2,1)}, bf16[2,256,1024]{2,1,0:T(8,128)(2,1)}, f32[1,2,4,1024]{3,2,1,0:T(4,128)}, f32[1,2,4,256]{3,2,1,0:T(4,128)}) custom-call(bf16[2,256,1024]{2,1,0:T(8,128)(2,1)} %tok.1, bf16[2,256,1024]{2,1,0:T(8,128)(2,1)} %cot.1, s32[2]{0:T(128)} %buckets.1, s32[2,8]{1,0:T(2,128)} %lengths.1, ...), custom_call_target="tpu_custom_call" | custom-call | tf_op jit(solution)/shard_map/two_layers/pallas_call | solution.py:1378
  226.9 2.5 %settle.1 = (bf16[1,2,256,1024]{3,2,1,0:T(8,128)(2,1)}, bf16[1,2,256,1024]{3,2,1,0:T(8,128)(2,1)}, f32[1,2,4,1024]{3,2,1,0:T(4,128)}, f32[1,2,4,256]{3,2,1,0:T(4,128)}) custom-call(bf16[2,256,1024]{2,1,0:T(8,128)(2,1)} %get-tuple-element.8.a_in, bf16[2,256,1024]{2,1,0:T(8,128)(2,1)} %get-tuple-element.9.g_in, f32[1,2,4,1024]{3,2,1,0:T(4,128)} %get-tuple-element.10.ta_in, ...), custom_call_target="tpu_custom_call" | custom-call | tf_op jit(solution)/shard_map/settle/pallas_call | solution.py:1355

commit v6 on v5

--- a/solution.py
+++ b/solution.py
@@ -510,7 +510,7 @@
                 src, dst, ws_s.at[p], ws_r.at[p], device_id=sib, device_id_type=MESH).start()
 
     def whole_by_y(l, p, c):
-        return l == 0 and p == 4 and c >= 2
+        return p == 4 and c >= 2
 
     def y_start(l, p):
         for c in range(pieces[p][2] if p else 1):
@@ -552,12 +552,6 @@
                 passed(l, p, c, z_half, sib, wa_s.at[k], wy_r.at[k]).wait_recv()
                 if p and not (p == 4 and c >= 2):
                     passed(l, p, c, z_half, zp, wz_s.at[k], wz_r.at[k]).start()
-
-                if p == 4 and c >= 2:
-
-                    @pl.when(l == 1)
-                    def _():
-                        passed(l, p, c, z_half, zp, wz_s.at[k], wz_r.at[k]).start()
 
                 passed(l, p, c, z_half, sib, wa_s.at[k], wa_r.at[k]).start()
 
@@ -1033,7 +1027,8 @@
             OACC[2 * k] = jnp.zeros(OACC.shape[1:], F32)
             OACC[2 * k + 1] = jnp.zeros(OACC.shape[1:], F32)
 
-        def turn(j, c):
+        def turn(step, c):
+            j = lax.rem(2 * b - step, b + 1)
             rows = pl.ds(pl.multiple_of(j * R, R), R)
             mask = MSK[pl.ds(pl.multiple_of((i * 2 + j) * R, R), R), :].astype(F32)
             for k in range(pairs):

time: 230 us -> 228 us (level)
  no operation moved by 1% of the time
where the time goes in v6:
time: 228 us; the launch traced here: 227 us
  Pallas kernels  227 us (100%)
    pallas_call x1, Pallas kernels, per_pair(): pl.pallas_call(partial(fused_kernel, dp_count), out_shape=(jax.ShapeDtype...  224 us

profile of v6, /device:TPU:0, one launch (start us, length us, event | category | flops | bytes accessed | tf_op | source)
XLA Modules:
  0.0 227.5 jit_solution(14199154306295903261)
XLA Ops:
  0.6 224.2 %two_layers.1 = (bf16[2,256,1024]{2,1,0:T(8,128)(2,1)}, bf16[2,256,1024]{2,1,0:T(8,128)(2,1)}, f32[1,2,4,1024]{3,2,1,0:T(4,128)}, f32[1,2,4,256]{3,2,1,0:T(4,128)}) custom-call(bf16[2,256,1024]{2,1,0:T(8,128)(2,1)} %tok.1, bf16[2,256,1024]{2,1,0:T(8,128)(2,1)} %cot.1, s32[2]{0:T(128)} %buckets.1, s32[2,8]{1,0:T(2,128)} %lengths.1, ...), custom_call_target="tpu_custom_call" | custom-call | tf_op jit(solution)/shard_map/two_layers/pallas_call | solution.py:1373
  224.8 2.5 %settle.1 = (bf16[1,2,256,1024]{3,2,1,0:T(8,128)(2,1)}, bf16[1,2,256,1024]{3,2,1,0:T(8,128)(2,1)}, f32[1,2,4,1024]{3,2,1,0:T(4,128)}, f32[1,2,4,256]{3,2,1,0:T(4,128)}) custom-call(bf16[2,256,1024]{2,1,0:T(8,128)(2,1)} %get-tuple-element.8.a_in, bf16[2,256,1024]{2,1,0:T(8,128)(2,1)} %get-tuple-element.9.g_in, f32[1,2,4,1024]{3,2,1,0:T(4,128)} %get-tuple-element.10.ta_in, ...), custom_call_target="tpu_custom_call" | custom-call | tf_op jit(solution)/shard_map/settle/pallas_call | solution.py:1350

commit v7 on v6

--- a/solution.py
+++ b/solution.py
@@ -1061,6 +1061,13 @@
                 def _():
                     dr_copy(k, k + 1).start()
 
+            @pl.when((s == 1) & (i == 0) & (j == 0))
+            def _():
+                dr_copy(0, b).wait_recv()
+                for q in range(4):
+                    BIG[q, pl.ds(pl.multiple_of(b * R, R), R), :] += DR[0, q]
+                dr_copy(0, 0).start()
+
             return c
 
         lax.fori_loop(0, b + 1, turn, 0)
@@ -1119,13 +1126,9 @@
                 for c in range(4):
                     BIG[c, own, :] += DR[k, c]
 
-            @pl.when(s == 1)
-            def _():
-                add(i)
-
-            @pl.when((s == 1) & (i == 0))
-            def _():
-                dr_copy(0, 0).start()
+            @pl.when((s == 1) & (i == 1))
+            def _():
+                add(1)
 
             @pl.when(s == 0)
             def _():

time: 228 us -> 226 us (level)
  no operation moved by 1% of the time
where the time goes in v7:
time: 226 us
  Pallas kernels  225 us (100%)
    pallas_call x1, Pallas kernels, per_pair(): pl.pallas_call(partial(fused_kernel, dp_count), out_shape=(jax.ShapeDtype...  222 us

profile of v7, /device:TPU:0, one launch (start us, length us, event | category | flops | bytes accessed | tf_op | source)
XLA Modules:
  0.0 225.6 jit_solution(11427619319778331171)
XLA Ops:
  0.6 222.3 %two_layers.1 = (bf16[2,256,1024]{2,1,0:T(8,128)(2,1)}, bf16[2,256,1024]{2,1,0:T(8,128)(2,1)}, f32[1,2,4,1024]{3,2,1,0:T(4,128)}, f32[1,2,4,256]{3,2,1,0:T(4,128)}) custom-call(bf16[2,256,1024]{2,1,0:T(8,128)(2,1)} %tok.1, bf16[2,256,1024]{2,1,0:T(8,128)(2,1)} %cot.1, s32[2]{0:T(128)} %buckets.1, s32[2,8]{1,0:T(2,128)} %lengths.1, ...), custom_call_target="tpu_custom_call" | custom-call | tf_op jit(solution)/shard_map/two_layers/pallas_call | solution.py:1376
  223.0 2.5 %settle.1 = (bf16[1,2,256,1024]{3,2,1,0:T(8,128)(2,1)}, bf16[1,2,256,1024]{3,2,1,0:T(8,128)(2,1)}, f32[1,2,4,1024]{3,2,1,0:T(4,128)}, f32[1,2,4,256]{3,2,1,0:T(4,128)}) custom-call(bf16[2,256,1024]{2,1,0:T(8,128)(2,1)} %get-tuple-element.8.a_in, bf16[2,256,1024]{2,1,0:T(8,128)(2,1)} %get-tuple-element.9.g_in, f32[1,2,4,1024]{3,2,1,0:T(4,128)} %get-tuple-element.10.ta_in, ...), custom_call_target="tpu_custom_call" | custom-call | tf_op jit(solution)/shard_map/settle/pallas_call | solution.py:1353
